TPU v7x, 32 devices: a whole 2x2x4 slice. The times are simulated.
32 devices in a mesh: dp: 8 (over z, x), tensor: 4 (over y, core).
Axes of the slice: x: 2, y: 2, z: 4, core: 2. Of those that a mesh axis runs over, the one named last changes fastest.
Arguments:
- block_input: float32 [32768, 512], P(('dp', 'tensor')), may hold values from -6 to 6
- long_rows: int32 [8], P('dp'), may hold values from 0 to 2, as said below
- short_rows: int32 [8], P('dp'), may hold values from 0 to 4, as said below
- prev_states: float32 [32, 1024], P('dp', 'tensor'), may hold values from 0 to 2
- norm1_gain: float32 [512], replicated, may hold values from 0.5 to 1.5
- conv_weight: float32 [4, 512], replicated, may hold values from -3 to 3
- mixer_weight: float32 [2, 512, 1024], P(None, None, 'tensor'), may hold values from -0.25 to 0.25
- gate_bias: float32 [1024], P('tensor'), may hold values from -7 to 1
- out_weight: float32 [1024, 512], P('tensor'), may hold values from -0.1875 to 0.1875
- norm2_gain: float32 [512], replicated, may hold values from 0.5 to 1.5
- up_weight: float32 [512, 2048], P(None, 'tensor'), may hold values from -0.25 to 0.25
- down_weight: float32 [2048, 512], P('tensor'), may hold values from -0.125 to 0.125
- cotangent: float32 [32768, 512], P(('dp', 'tensor')), may hold values from -6 to 6
Outputs:
- output: float32 [32768, 512], P(('dp', 'tensor'))
- final_states: float32 [32, 1024], P('dp', 'tensor')
- input_grad: float32 [32768, 512], P(('dp', 'tensor'))
- norm1_gain_grad: float32 [512], replicated
- conv_weight_grad: float32 [4, 512], replicated
- mixer_weight_grad: float32 [2, 512, 1024], P(None, None, 'tensor')
- gate_bias_grad: float32 [1024], P('tensor')
- out_weight_grad: float32 [1024, 512], P('tensor')
- norm2_gain_grad: float32 [512], replicated
- up_weight_grad: float32 [512, 2048], P(None, 'tensor')
- down_weight_grad: float32 [2048, 512], P('tensor')
Inputs may be any that keep to these rules, and one draw needn't show every extreme that they name: In each group 2048 long_rows + 1024 short_rows lies between half of 4096 and 4096; in every draw one group is filled by long rows alone and another by short rows alone. `short_rows`: see long_rows.
All inputs are finite; a program needn't handle non-finite values.
Results may differ from a plain program's by a relative error of at most 0.0084.
Values may be sent and summed in bfloat16 or wider, within the bound.
A program may use at most 320 MiB of HBM per device.

v0:
```python
import jax
import jax.numpy as jnp
from jax import lax
from jax.sharding import PartitionSpec as P

SHORT = 1024
LONG = 2048


epsilon = 1e-06
highest = lax.Precision.HIGHEST


def from_behind(shard, axis, by):
    count = lax.axis_size(axis)
    pairs = [(i, i + by) for i in range(count) if 0 <= i + by < count]
    return lax.ppermute(shard, axis, pairs)


def rms_norm(values, gain):
    return values * lax.rsqrt(jnp.mean(values * values, axis=-1, keepdims=True) + epsilon) * gain


def combine(before_pair, after_pair):
    return (before_pair[0] * after_pair[0], after_pair[0] * before_pair[1] + after_pair[1])


def prefix_scan(factors, values):
    length = factors.shape[0]
    columns = factors.shape[1]
    if length <= 8:
        factor_list = [factors[0]]
        value_list = [values[0]]
        for step in range(1, length):
            factor_list.append(factors[step] * factor_list[-1])
            value_list.append(factors[step] * value_list[-1] + values[step])
        return (jnp.stack(factor_list, 0), jnp.stack(value_list, 0))
    block_size = 0
    for candidate in (8, 4, 2):
        if block_size == 0 and length % candidate == 0:
            block_size = candidate
    if block_size == 0:
        return lax.associative_scan(combine, (factors, values), axis=0)
    blocks = length // block_size
    factor_blocks = factors.reshape(blocks, block_size, columns)
    value_blocks = values.reshape(blocks, block_size, columns)
    factor_list = [factor_blocks[:, 0]]
    value_list = [value_blocks[:, 0]]
    for step in range(1, block_size):
        factor_list.append(factor_blocks[:, step] * factor_list[-1])
        value_list.append(factor_blocks[:, step] * value_list[-1] + value_blocks[:, step])
    inner_factor = jnp.stack(factor_list, 1)
    inner_value = jnp.stack(value_list, 1)
    outer_factor, outer_value = prefix_scan(factor_list[-1], value_list[-1])
    prior_factor = jnp.concatenate([jnp.ones((1, columns), factors.dtype), outer_factor[:-1]], 0)
    prior_value = jnp.concatenate([jnp.zeros((1, columns), values.dtype), outer_value[:-1]], 0)
    total_factor = inner_factor * prior_factor[:, None]
    total_value = inner_factor * prior_value[:, None] + inner_value
    return (total_factor.reshape(length, columns), total_value.reshape(length, columns))


def gelu_tanh(values):
    return jax.nn.gelu(values, approximate=True)


def matmul(left, right):
    return jnp.dot(left, right, preferred_element_type=jnp.float32)


def left_contract(left, right):
    return lax.dot_general(
        left, right, (((0,), (0,)), ((), ())), preferred_element_type=jnp.float32
    )


def right_contract(left, right):
    return lax.dot_general(
        left, right, (((1,), (1,)), ((), ())), preferred_element_type=jnp.float32
    )


def layout(long_rows, short_rows, group_tokens):
    token = jnp.arange(group_tokens, dtype=jnp.int32)[None, :]
    long_count = long_rows[:, None]
    short_count = short_rows[:, None]
    long_end = LONG * long_count
    short_end = long_end + SHORT * short_count
    in_long = token < long_end
    in_short = (token >= long_end) & (token < short_end)
    position = jnp.where(in_long, token % LONG, jnp.where(in_short, (token - long_end) % SHORT, 0))
    slot_index = jnp.where(
        in_long, token // LONG, jnp.where(in_short, long_count + (token - long_end) // SHORT, -1)
    )
    length = jnp.where(in_long, LONG, SHORT)
    in_row = in_long | in_short
    row_end = in_row & (position == length - 1)
    return (position[0], slot_index[0], in_row[0], row_end[0])


def per_device(
    block_input,
    long_rows,
    short_rows,
    prev_states,
    norm1_gain,
    conv_weight,
    mixer_weight,
    gate_bias,
    out_weight,
    norm2_gain,
    up_weight,
    down_weight,
    cotangent,
):
    local_tokens, width = block_input.shape
    part_count = lax.axis_size("tensor")
    group_tokens = local_tokens * part_count
    slot_count = prev_states.shape[0]
    channels = gate_bias.shape[0]
    rim_rows = conv_weight.shape[0] - 1
    position, slot_index, in_row, row_end = layout(long_rows, short_rows, group_tokens)
    offset = lax.axis_index("tensor") * local_tokens
    local_position = lax.dynamic_slice_in_dim(position, offset, local_tokens)
    local_mask = lax.dynamic_slice_in_dim(in_row, offset, local_tokens).astype(jnp.float32)[:, None]
    slot_table = (slot_index[:, None] == jnp.arange(slot_count, dtype=jnp.int32)).astype(
        jnp.float32
    )
    end_table = slot_table * row_end[:, None].astype(jnp.float32)
    start = (in_row & (position == 0)).astype(jnp.float32)[:, None]
    linked = (in_row & (position > 0)).astype(jnp.float32)[:, None]

    def convolve(extended, weight):
        total = jnp.zeros((local_tokens, width), jnp.float32)
        for tap_index in range(weight.shape[0]):
            window = extended[rim_rows - tap_index : rim_rows - tap_index + local_tokens]
            total = total + weight[tap_index] * window * (local_position >= tap_index)[
                :, None
            ].astype(jnp.float32)
        return total

    normed, norm1_back = jax.vjp(rms_norm, block_input, norm1_gain)
    rim_input = from_behind(normed[local_tokens - rim_rows :], "tensor", 1)
    conv_out, conv_back = jax.vjp(convolve, jnp.concatenate([rim_input, normed], 0), conv_weight)
    conv_low = conv_out.astype(jnp.bfloat16)
    mixer_cols = jnp.concatenate([mixer_weight[0], mixer_weight[1]], 1).astype(jnp.bfloat16)
    out_low = out_weight.astype(jnp.bfloat16)
    seed_state = (
        jnp.dot(slot_table, prev_states, precision=highest, preferred_element_type=jnp.float32)
        * start
    )

    def recurrence(projected, bias):
        logit = projected[:, :channels] + bias
        keep = jax.nn.sigmoid(-logit)
        update = jax.nn.sigmoid(logit) * jax.nn.softplus(projected[:, channels:])
        _, states = prefix_scan(keep * linked, update + keep * seed_state)
        return states

    conv_full = lax.all_gather(conv_low, "tensor", axis=0, tiled=True)
    projected = matmul(conv_full, mixer_cols)
    states, recur_back = jax.vjp(recurrence, projected, gate_bias)
    finals = jnp.einsum("ts,tc->sc", end_table, states, precision=highest)
    state_low = states.astype(jnp.bfloat16)
    mixed = lax.psum_scatter(
        matmul(
            lax.slice_in_dim(state_low, 0, local_tokens * lax.axis_size("tensor"), axis=0), out_low
        ),
        "tensor",
        scatter_dimension=0,
        tiled=True,
    )
    resid = block_input + local_mask * mixed
    normed_two, norm2_back = jax.vjp(rms_norm, resid, norm2_gain)
    normed_low = normed_two.astype(jnp.bfloat16)
    up_low = up_weight.astype(jnp.bfloat16)
    down_low = down_weight.astype(jnp.bfloat16)
    grad_branch = (local_mask * cotangent).astype(jnp.bfloat16)
    up_full, down_full = (
        lax.all_gather(up_low, "tensor", axis=1, tiled=True),
        lax.all_gather(down_low, "tensor", axis=0, tiled=True),
    )
    upward = matmul(normed_low, up_full)
    activation, gelu_back = jax.vjp(gelu_tanh, upward)
    activation_low = activation.astype(jnp.bfloat16)
    output = resid + local_mask * matmul(activation_low, down_full)
    grad_act = right_contract(grad_branch, down_full)
    grad_up = gelu_back(grad_act)[0].astype(jnp.bfloat16)
    grad_norm_two = right_contract(grad_up, up_full)
    up_grad, down_grad = (
        lax.psum_scatter(
            left_contract(normed_low, grad_up), "tensor", scatter_dimension=1, tiled=True
        ),
        lax.psum_scatter(
            left_contract(activation_low, grad_branch), "tensor", scatter_dimension=0, tiled=True
        ),
    )
    grad_resid_norm, gain_two_part = norm2_back(grad_norm_two)
    grad_resid = cotangent + grad_resid_norm
    grad_mixed = (local_mask * grad_resid).astype(jnp.bfloat16)
    grad_mixed_full = lax.all_gather(grad_mixed, "tensor", axis=0, tiled=True)
    out_grad = left_contract(state_low, grad_mixed_full)
    grad_states = right_contract(grad_mixed_full, out_low)
    grad_projected, bias_part = recur_back(grad_states)
    grad_proj_low = grad_projected.astype(jnp.bfloat16)
    mixer_grad_cols = left_contract(conv_full, grad_proj_low)
    mixer_grad = jnp.stack([mixer_grad_cols[:, :channels], mixer_grad_cols[:, channels:]])
    grad_conv = lax.psum_scatter(
        right_contract(
            lax.slice_in_dim(grad_proj_low, 0, local_tokens * lax.axis_size("tensor"), axis=0),
            mixer_cols,
        ),
        "tensor",
        scatter_dimension=0,
        tiled=True,
    )
    grad_extended, taps_part = conv_back(grad_conv)
    returned = from_behind(grad_extended[:rim_rows], "tensor", -1)
    grad_normed = grad_extended[rim_rows:] + jnp.concatenate(
        [jnp.zeros((local_tokens - rim_rows, width), jnp.float32), returned], 0
    )
    grad_input_norm, gain_one_part = norm1_back(grad_normed)
    input_grad = grad_resid + grad_input_norm
    summed = lax.psum((mixer_grad, bias_part, out_grad, up_grad, down_grad), "dp")
    shared = lax.psum((gain_one_part, taps_part, gain_two_part), ("dp", "tensor"))
    return (
        output,
        finals,
        input_grad,
        shared[0],
        shared[1],
        summed[0],
        summed[1],
        summed[2],
        shared[2],
        summed[3],
        summed[4],
    )


def solution(mesh):
    placed = (
        P(("dp", "tensor"), None),
        P("dp"),
        P("dp"),
        P("dp", "tensor"),
        P(),
        P(),
        P(None, None, "tensor"),
        P("tensor"),
        P("tensor", None),
        P(),
        P(None, "tensor"),
        P("tensor", None),
        P(("dp", "tensor"), None),
    )
    return jax.shard_map(
        per_device,
        mesh=mesh,
        in_specs=placed,
        out_specs=(
            P(("dp", "tensor"), None),
            P("dp", "tensor"),
            P(("dp", "tensor"), None),
            P(),
            P(),
            P(None, None, "tensor"),
            P("tensor"),
            P("tensor", None),
            P(),
            P(None, "tensor"),
            P("tensor", None),
        ),
        check_vma=False,
    )
```

profile of v0, /device:TPU:0, one launch (start us, length us, event | category | flops | bytes accessed | tf_op | source)
XLA Modules:
  0.0 611.3 jit_solution(12417529751389112777)
XLA Ops:
  7.2 1.8 multiply_reduce_fusion.10
  10.3 1.9 multiply_multiply_fusion.6
  12.2 2.4 collective-permute-start
  17.3 2.3 add_convert_fusion.1
  20.0 3.8 convolution_multiply_fusion
  23.8 33.1 %all-gather.5.cloned.1.call-done = bf16[4096,512]{1,0:T(8,128)(2,1)} async-done(((bf16[1024,512]{1,0:T(8,128)(2,1)}), bf16[4096,512]{1,0:T(8,128)(2,1)}) %all-gather.5.cloned.1.call-update) | async-done | bytes 4194320 | tf_op jit(solution)/shard_map/all_gather | solution.py:159
  56.9 4.7 fusion.26
  61.6 4.0 multiply_bitcast_fusion
  65.7 2.8 fusion.117
  68.6 2.8 fusion.118
  71.5 2.8 fusion.27
  84.0 2.3 stack.22
  86.3 2.5 stack.19
  98.3 2.0 copy-done.8
  100.4 5.9 fusion.23
  106.4 2.2 convert_element_type.127
  108.7 2.1 convert_element_type.129
  110.8 67.3 %reduce-scatter.5.cloned.1.call-done = f32[1024,512]{1,0:T(8,128)} async-done(((f32[4096,512]{1,0:T(8,128)}), f32[1024,512]{1,0:T(8,128)}) %reduce-scatter.5.cloned.1.call-update) | async-done | bytes 2097168 | tf_op jit(solution)/shard_map/reduce_scatter | solution.py:164
  178.2 3.4 multiply_reduce_fusion.9
  182.1 20.3 %all-gather.7.cloned.1.call-done = bf16[512,2048]{1,0:T(8,128)(2,1)} async-done(((bf16[512,512]{1,0:T(8,128)(2,1)}), bf16[512,2048]{1,0:T(8,128)(2,1)}) %all-gather.7.cloned.1.call-update) | async-done | bytes 2097168 | tf_op jit(solution)/shard_map/all_gather | solution.py:179
  202.4 7.9 %fusion.96 = f32[1024,2048]{1,0:T(8,128)} fusion(bf16[512,2048]{1,0:T(8,128)(2,1)} %all-gather.7.cloned.1.call-done, f32[1024,512]{1,0:T(8,128)} %get-tuple-element.94, f32[512]{0:T(512)S(1)} %copy-done.115, f32[1024]{0:T(1024)S(1)} %fusion.78), kind=kOutput, calls=%fused_computation.398 | convolution fusion | flops 2149056512 | bytes 12589056 | tf_op jit(solution)/shard_map/dot_general | solution.py:67
  210.4 16.7 %all-gather.9.cloned.1.call-done = bf16[2048,512]{1,0:T(8,128)(2,1)} async-done(((bf16[512,512]{1,0:T(8,128)(2,1)}), bf16[2048,512]{1,0:T(8,128)(2,1)}) %all-gather.9.cloned.1.call-update) | async-done | bytes 2097168 | tf_op jit(solution)/shard_map/all_gather | solution.py:180
  227.1 10.4 %fusion.6 = bf16[1024,2048]{1,0:T(8,128)(2,1)S(1)} fusion(f32[1024,2048]{1,0:T(8,128)} %fusion.96, bf16[2048,512]{1,0:T(8,128)(2,1)} %all-gather.9.cloned.1.call-done, f32[1024,512]{1,0:T(8,128)} %param.25, f32[1024]{0:T(1024)} %bitcast.455), kind=kOutput, calls=%fused_computation.11 | convolution fusion | flops 2190475264 | bytes 16781312 | tf_op jit(solution)/shard_map/dot_general | solution.py:77
  237.6 3.2 multiply_reduce_fusion.1
  240.8 2.2 multiply_convert_fusion.1
  243.2 9.9 %fusion.88 = f32[2048,512]{1,0:T(8,128)} fusion(f32[1024,512]{1,0:T(8,128)} %param.25, f32[1024]{0:T(1024)} %bitcast.456, f32[1024,2048]{1,0:T(8,128)} %fusion.96), kind=kOutput, calls=%fused_computation.390 | convolution fusion | flops 2167406592 | bytes 14684160 | tf_op jit(solution)/shard_map/dot_general | solution.py:71
  253.1 7.3 %fusion.95 = f32[512,2048]{1,0:T(8,128)} fusion(bf16[1024,2048]{1,0:T(8,128)(2,1)} %copy-done.21, f32[1024,512]{1,0:T(8,128)} %get-tuple-element.94, f32[512]{0:T(512)S(1)} %copy-done.115, f32[1024]{0:T(1024)S(1)} %fusion.78), kind=kOutput, calls=%fused_computation.397 | convolution fusion | flops 2149056512 | bytes 10491904 | tf_op jit(solution)/shard_map/dot_general | solution.py:71
  260.7 17.0 %all-gather.11.cloned.1.call-done = bf16[4096,512]{1,0:T(8,128)(2,1)} async-done(((bf16[1024,512]{1,0:T(8,128)(2,1)}), bf16[4096,512]{1,0:T(8,128)(2,1)}) %all-gather.11.cloned.1.call-update) | async-done | bytes 4194320 | tf_op jit(solution)/shard_map/all_gather | solution.py:200
  277.7 3.7 convolution_bitcast_fusion
  281.5 2.5 fusion.116
  303.7 10.6 %fusion.97 = (f32[256]{0:T(256)S(1)}, f32[4096,256]{1,0:T(8,128)S(1)}, f32[4096,256]{1,0:T(8,128)S(1)}) fusion(f32[4096]{0:T(1024)S(1)} %copy-done.104, f32[512,8,256]{2,0,1:T(8,128)S(1)} %pad_add_fusion, f32[4096,256]{1,0:T(8,128)S(1)} %copy-done.7, f32[256]{0:T(256)S(1)} %copy-done.155, f32[4096,512]{1,0:T(8,128)S(1)} %bitcast.440, ...), kind=kLoop, calls=%fused_computation.399 | loop fusion | flops 33554176 | bytes 29378560 | tf_op jit(solution)/shard_map/transpose(jvp())/reduce_sum | solution.py:153
  314.3 2.1 copy-done.58
  317.7 5.8 fusion.25
  323.7 7.2 %fusion.24 = f32[512,512]{1,0:T(8,128)S(1)} fusion(bf16[4096,512]{1,0:T(8,128)(2,1)} %all-gather.5.cloned.1.call-done, f32[4096,256]{1,0:T(8,128)} %copy-done.58, f32[4096,256]{1,0:T(8,128)} %copy-done.59), kind=kOutput, calls=%fused_computation.79 | convolution fusion | flops 2151677952 | bytes 13631488 | tf_op jit(solution)/shard_map/dot_general | solution.py:71
  332.1 2.1 copy-done.9
  334.2 3.9 fusion.22
  338.1 33.8 %reduce-scatter.9.cloned.1.call-done = f32[512,512]{1,0:T(8,128)} async-done(((f32[512,2048]{1,0:T(8,128)}), f32[512,512]{1,0:T(8,128)}) %reduce-scatter.9.cloned.1.call-update) | async-done | bytes 1048592 | tf_op jit(solution)/shard_map/reduce_scatter | solution.py:190
  372.0 6.8 %fusion.15 = f32[4,256]{1,0:T(4,128)} fusion(f32[512,8,256]{2,0,1:T(8,128)} %copy-done.8, f32[4096]{0:T(1024)S(1)} %fusion.56, s32[4096]{0:T(1024)S(1)} %copy-done.106), kind=kOutput, calls=%fused_computation.30 | convolution fusion | flops 50364416 | bytes 4231168 | tf_op jit(solution)/shard_map/ts,tc->sc/dot_general | solution.py:162
  378.9 8.6 %multiply_add_fusion.1 = f32[1024,512]{1,0:T(8,128)} fusion(f32[1024,512]{1,0:T(8,128)S(1)} %copy-done.5, bf16[2048,512]{1,0:T(8,128)(2,1)S(1)} %copy-done.157, f32[1024]{0:T(1024)S(1)} %bitcast.459, f32[1024,2048]{1,0:T(8,128)} %fusion.96), kind=kOutput, calls=%fused_computation.64 | convolution fusion | flops 2167406592 | bytes 14684160 | tf_op jit(solution)/shard_map/dot_general | solution.py:67
  387.5 22.0 %psum.59 = f32[256]{0:T(256)} all-reduce(f32[256]{0:T(256)S(1)} %get-tuple-element.26), channel_id=1, replica_groups=mesh['dp'=8,'tensor'=4] {'dp'}, use_global_device_ids=true, to_apply=%region_18.19 | all-reduce | flops 256 | bytes 2048 | tf_op jit(solution)/shard_map/psum | solution.py:223
  409.5 37.0 %reduce-scatter.7.cloned.1.call-done = f32[1024,512]{1,0:T(8,128)} async-done(((f32[4096,512]{1,0:T(8,128)}), f32[1024,512]{1,0:T(8,128)}) %reduce-scatter.7.cloned.1.call-update) | async-done | bytes 2097168 | tf_op jit(solution)/shard_map/reduce_scatter | solution.py:207
  446.5 6.6 %multiply_reduce_fusion.5 = (f32[512]{0:T(512)S(1)}, f32[512]{0:T(512)S(1)}, f32[512]{0:T(512)S(1)}, f32[512]{0:T(512)S(1)}, f32[1024,512]{1,0:T(8,128)S(1)}, /*...) fusion(f32[1024,512]{1,0:T(8,128)} %reduce-scatter.7.cloned.1.call-done, ...), kind=kLoop, calls=%fused_computation.58 | loop fusion | flops 9959424 | bytes 12621824 | tf_op jit(solution)/shard_map/transpose(jvp())/reduce_sum | solution.py:136
  457.9 44.7 %all-reduce.98 = (f32[512]{0:T(512)}, f32[4,512]{1,0:T(4,128)}, f32[512]{0:T(512)}) all-reduce(f32[512]{0:T(512)S(1)} %get-tuple-element.11, f32[4,512]{1,0:T(4,128)S(1)} %pad_add_fusion.6, f32[512]{0:T(512)S(1)} %copy-done.156), channel_id=1, replica_groups=mesh['dp'=8,'tensor'=4] {'dp','tensor'}, use_global_device_ids=true, to_apply=%region_10.11 | all-reduce | flops 3072 | bytes 24576 | tf_op jit(solution)/shard_map/psum | solution.py:224
  502.5 4.2 fusion.21
  506.7 90.2 %all-reduce.102.cloned.1.call-done = (f32[2,512,256]{2,1,0:T(8,128)}, f32[256,512]{1,0:T(8,128)}, f32[512,512]{1,0:T(8,128)}, f32[512,512]{1,0:T(8,128)}) async-done(((f32[2,512,256]{2,1,0:T(8,128)}, f32[256,512]{1,0:T(8,128)}, f32[512,512]{1,0:T(8,128)}, f32[512,512]{1,0:T(8,128)}), (f32[2,512,256]{2,1,0:T(8,128)}, f32[256,512]{1,0:T(8,128)}, f32[512,512]{1,0:T(8,128)}, ...) | async-done | bytes 3670032 | tf_op jit(solution)/shard_map/psum | solution.py:223
  596.9 2.4 copy.836
  599.2 1.9 copy.837
  601.1 2.3 copy.838
  (457 shorter events, 49.9 us)
Async XLA Ops:
  7.2 12.8 %copy-start = (f32[4,256]{1,0:T(4,128)S(1)}, f32[4,256]{1,0:T(4,128)}, u32[]{:S(2)}) copy-start(f32[4,256]{1,0:T(4,128)} %param.16) | copy-start | bytes 12292
  7.2 8.8 %copy-start.153 = (f32[4,512]{1,0:T(4,128)S(1)}, f32[4,512]{1,0:T(4,128)}, u32[]{:S(2)}) copy-start(f32[4,512]{1,0:T(4,128)} %param.18) | copy-start | bytes 24580
  7.2 49.7 %all-gather.5.cloned.1.call-start = ((), (), s32[]{:S(2)}) async-start(), calls=%async_computation.4 | async-start | bytes 5242880 | tf_op jit(solution)/shard_map/all_gather | solution.py:159
  10.3 9.5 %copy-start.64 = (f32[2,512,256]{2,1,0:T(8,128)S(1)}, f32[2,512,256]{2,1,0:T(8,128)}, u32[]{:S(2)}) copy-start(f32[2,512,256]{2,1,0:T(8,128)} %param.19) | copy-start | bytes 3145732
  12.2 11.6 %copy-start.13 = (f32[1024,512]{1,0:T(8,128)}, f32[1024,512]{1,0:T(8,128)S(1)}, u32[]{:S(2)}) copy-start(f32[1024,512]{1,0:T(8,128)S(1)} %multiply_multiply_fusion.6) | copy-start | bytes 6291460
  12.2 4.6 collective-permute-start
  19.7 158.5 %reduce-scatter.5.cloned.1.call-start = ((), (), s32[]{:S(2)}) async-start(), calls=%async_computation.5 | async-start | bytes 10485760 | tf_op jit(solution)/shard_map/reduce_scatter | solution.py:164
  19.8 41.8 %copy-start.103 = (f32[4096]{0:T(1024)}, f32[4096]{0:T(1024)S(1)}, u32[]{:S(2)}) copy-start(f32[4096]{0:T(1024)S(1)} %and_convert_fusion.1) | copy-start | bytes 49156
  19.9 41.7 %copy-start.105 = (s32[4096]{0:T(1024)}, s32[4096]{0:T(1024)S(1)}, u32[]{:S(2)}) copy-start(s32[4096]{0:T(1024)S(1)} %fusion.40) | copy-start | bytes 49156
  20.0 41.6 %copy-start.66 = (bf16[512,256]{1,0:T(8,128)(2,1)}, bf16[512,256]{1,0:T(8,128)(2,1)S(1)}, u32[]{:S(2)}) copy-start(bf16[512,256]{1,0:T(8,128)(2,1)S(1)} %get-tuple-element.189) | copy-start | bytes 786436
  68.6 27.4 %copy-start.17 = (f32[512,1,256]{2,1,0:T(1,128)}, f32[512,1,256]{2,1,0:T(1,128)S(1)}, u32[]{:S(2)}) copy-start(f32[512,1,256]{2,1,0:T(1,128)S(1)} %get-tuple-element.156) | copy-start | bytes 1572868
  74.3 16.0 %copy-start.22 = (f32[64,8,256]{2,1,0:T(8,128)}, f32[64,8,256]{2,1,0:T(8,128)S(1)}, u32[]{:S(2)}) copy-start(f32[64,8,256]{2,1,0:T(8,128)S(1)} %get-tuple-element.126) | copy-start | bytes 1572868
  74.3 16.9 %copy-start.15 = (f32[512,1,256]{2,0,1:T(8,128)}, f32[512,1,256]{2,0,1:T(8,128)S(1)}, u32[]{:S(2)}) copy-start(f32[512,1,256]{2,0,1:T(8,128)S(1)} %get-tuple-element.130) | copy-start | bytes 1572868
  74.3 18.5 %copy-start.19 = (f32[512,1,256]{2,0,1:T(8,128)}, f32[512,1,256]{2,0,1:T(8,128)S(1)}, u32[]{:S(2)}) copy-start(f32[512,1,256]{2,0,1:T(8,128)S(1)} %get-tuple-element.129) | copy-start | bytes 1572868
  79.8 12.3 %copy-start.146 = (f32[1,256]{1,0:T(1,128)}, f32[1,256]{1,0:T(1,128)S(1)}, u32[]{:S(2)}) copy-start(f32[1,256]{1,0:T(1,128)S(1)} %get-tuple-element.90) | copy-start | bytes 3076
  79.8 12.3 %copy-start.148 = (f32[1,256]{1,0:T(1,128)}, f32[1,256]{1,0:T(1,128)S(1)}, u32[]{:S(2)}) copy-start(f32[1,256]{1,0:T(1,128)S(1)} %get-tuple-element.89) | copy-start | bytes 3076
  106.3 71.9 %copy-start.3 = (f32[1024,512]{1,0:T(8,128)S(1)}, f32[1024,512]{1,0:T(8,128)}, u32[]{:S(2)}) copy-start(f32[1024,512]{1,0:T(8,128)} %param.13) | copy-start | bytes 6291460
  106.3 71.9 %copy-start.118 = (f32[1,1024]{1,0:T(1,128)S(1)}, f32[1,1024]{1,0:T(1,128)}, u32[]{:S(2)}) copy-start(f32[1,1024]{1,0:T(1,128)} %get-tuple-element.220) | copy-start | bytes 12292
  106.3 96.1 %all-gather.7.cloned.1.call-start = ((), (), s32[]{:S(2)}) async-start(), calls=%async_computation.6 | async-start | bytes 2621440 | tf_op jit(solution)/shard_map/all_gather | solution.py:179
  108.6 93.8 %copy-start.115 = (f32[512]{0:T(512)S(1)}, f32[512]{0:T(512)}, u32[]{:S(2)}) copy-start(f32[512]{0:T(512)} %param.22) | copy-start | bytes 6148
  108.6 118.5 %all-gather.9.cloned.1.call-start = ((), (), s32[]{:S(2)}) async-start(), calls=%async_computation.7 | async-start | bytes 2621440 | tf_op jit(solution)/shard_map/all_gather | solution.py:180
  110.8 167.0 %all-gather.11.cloned.1.call-start = ((), (), s32[]{:S(2)}) async-start(), calls=%async_computation.8 | async-start | bytes 5242880 | tf_op jit(solution)/shard_map/all_gather | solution.py:200
  227.1 10.4 %copy-start.4 = (f32[1024,512]{1,0:T(8,128)S(1)}, f32[1024,512]{1,0:T(8,128)}, u32[]{:S(2)}) copy-start(f32[1024,512]{1,0:T(8,128)} %get-tuple-element.94) | copy-start | bytes 6291460
  227.1 10.4 %copy-start.63 = (bf16[512,2048]{1,0:T(8,128)(2,1)S(1)}, bf16[512,2048]{1,0:T(8,128)(2,1)}, u32[]{:S(2)}) copy-start(bf16[512,2048]{1,0:T(8,128)(2,1)} %all-gather.7.cloned.1.call-done) | copy-start | bytes 6291460
  243.1 95.0 %reduce-scatter.11.cloned.1.call-start = ((), (), s32[]{:S(2)}) async-start(), calls=%async_computation.11 | async-start | bytes 5242880 | tf_op jit(solution)/shard_map/reduce_scatter | solution.py:193
  253.1 118.8 %reduce-scatter.9.cloned.1.call-start = ((), (), s32[]{:S(2)}) async-start(), calls=%async_computation.10 | async-start | bytes 5242880 | tf_op jit(solution)/shard_map/reduce_scatter | solution.py:190
  260.5 186.0 %reduce-scatter.7.cloned.1.call-start = ((), (), s32[]{:S(2)}) async-start(), calls=%async_computation.9 | async-start | bytes 10485760 | tf_op jit(solution)/shard_map/reduce_scatter | solution.py:207
  284.3 6.2 %copy-start.76 = (f32[64,1,256]{2,1,0:T(1,128)S(1)}, f32[64,1,256]{2,1,0:T(1,128)}, u32[]{:S(2)}) copy-start(f32[64,1,256]{2,1,0:T(1,128)} %get-tuple-element.118) | copy-start | bytes 196612
  303.7 14.0 %copy-start.67 = (bf16[512,256]{1,0:T(8,128)(2,1)S(1)}, bf16[512,256]{1,0:T(8,128)(2,1)}, u32[]{:S(2)}) copy-start(bf16[512,256]{1,0:T(8,128)(2,1)} %copy-done.66) | copy-start | bytes 786436
  323.5 273.4 %all-reduce.102.cloned.1.call-start = ((), (), s32[]{:S(2)}) async-start(), calls=%async_computation.12 | async-start | bytes 7340032 | tf_op jit(solution)/shard_map/psum | solution.py:223
  323.7 8.4 %copy-start.36 = (bf16[4096,512]{1,0:T(8,128)(2,1)S(1)}, bf16[4096,512]{1,0:T(8,128)(2,1)}, u32[]{:S(2)}) copy-start(bf16[4096,512]{1,0:T(8,128)(2,1)} %all-gather.11.cloned.1.call-done) | copy-start | bytes 12582916
  334.2 37.8 %copy-start.106 = (s32[4096]{0:T(1024)S(1)}, s32[4096]{0:T(1024)}, u32[]{:S(2)}) copy-start(s32[4096]{0:T(1024)} %copy-done.105) | copy-start | bytes 49156
  338.1 40.7 %copy-start.120 = (f32[1,1024]{1,0:T(1,128)S(1)}, f32[1,1024]{1,0:T(1,128)}, u32[]{:S(2)}) copy-start(f32[1,1024]{1,0:T(1,128)} %get-tuple-element.220) | copy-start | bytes 12292
  372.0 6.9 %copy-start.5 = (f32[1024,512]{1,0:T(8,128)S(1)}, f32[1024,512]{1,0:T(8,128)}, u32[]{:S(2)}) copy-start(f32[1024,512]{1,0:T(8,128)} %get-tuple-element.94) | copy-start | bytes 6291460
  372.0 6.9 %copy-start.157 = (bf16[2048,512]{1,0:T(8,128)(2,1)S(1)}, bf16[2048,512]{1,0:T(8,128)(2,1)}, u32[]{:S(2)}) copy-start(bf16[2048,512]{1,0:T(8,128)(2,1)} %all-gather.9.cloned.1.call-done) | copy-start | bytes 6291460
  378.8 67.6 %copy-start.117 = (f32[1,1024]{1,0:T(1,128)S(1)}, f32[1,1024]{1,0:T(1,128)}, u32[]{:S(2)}) copy-start(f32[1,1024]{1,0:T(1,128)} %copy-done.116) | copy-start | bytes 12292
  378.8 67.6 %copy-start.122 = (f32[1,1024]{1,0:T(1,128)S(1)}, f32[1,1024]{1,0:T(1,128)}, u32[]{:S(2)}) copy-start(f32[1,1024]{1,0:T(1,128)} %copy-done.121) | copy-start | bytes 12292
  378.8 67.6 %copy-start.124 = (f32[1,1024]{1,0:T(1,128)S(1)}, f32[1,1024]{1,0:T(1,128)}, u32[]{:S(2)}) copy-start(f32[1,1024]{1,0:T(1,128)} %copy-done.123) | copy-start | bytes 12292
  378.8 67.6 %copy-start.126 = (f32[1,1024]{1,0:T(1,128)S(1)}, f32[1,1024]{1,0:T(1,128)}, u32[]{:S(2)}) copy-start(f32[1,1024]{1,0:T(1,128)} %copy-done.125) | copy-start | bytes 12292
  378.9 67.6 %copy-start.135 = (f32[3,512]{1,0:T(4,128)S(1)}, f32[3,512]{1,0:T(4,128)}, u32[]{:S(2)}) copy-start(f32[3,512]{1,0:T(4,128)} %copy-done.134) | copy-start | bytes 18436
  378.9 67.6 %copy-start.138 = (f32[1,512]{1,0:T(1,128)S(1)}, f32[1,512]{1,0:T(1,128)}, u32[]{:S(2)}) copy-start(f32[1,512]{1,0:T(1,128)} %copy-done.137) | copy-start | bytes 6148
  378.9 67.6 %copy-start.140 = (f32[1,512]{1,0:T(1,128)S(1)}, f32[1,512]{1,0:T(1,128)}, u32[]{:S(2)}) copy-start(f32[1,512]{1,0:T(1,128)} %copy-done.139) | copy-start | bytes 6148
  378.9 67.6 %copy-start.142 = (f32[1,512]{1,0:T(1,128)S(1)}, f32[1,512]{1,0:T(1,128)}, u32[]{:S(2)}) copy-start(f32[1,512]{1,0:T(1,128)} %copy-done.141) | copy-start | bytes 6148
  378.9 67.6 %copy-start.144 = (f32[1,512]{1,0:T(1,128)S(1)}, f32[1,512]{1,0:T(1,128)}, u32[]{:S(2)}) copy-start(f32[1,512]{1,0:T(1,128)} %copy-done.143) | copy-start | bytes 6148
  453.1 3.1 collective-permute-start.1
  455.5 47.0 %copy-start.128 = (f32[1024]{0:T(1024)S(1)}, f32[1024]{0:T(1024)}, u32[]{:S(2)}) copy-start(f32[1024]{0:T(1024)} %copy-done.127) | copy-start | bytes 12292
  502.5 101.8 %copy-start.1 = (f32[4,256]{1,0:T(4,128)S(1)}, f32[4,256]{1,0:T(4,128)}, u32[]{:S(2)}) copy-start(f32[4,256]{1,0:T(4,128)} %param.16) | copy-start | bytes 12292
  596.9 6.5 %copy-start.65 = (f32[512,512]{1,0:T(8,128)S(1)}, f32[512,512]{1,0:T(8,128)}, u32[]{:S(2)}) copy-start(f32[512,512]{1,0:T(8,128)} %get-tuple-element.259) | copy-start | bytes 3145732
  (123 other events, 414.1 us)
Sparse Core Ops, SparseCore 0:
  19.8 37.0 all-gather.4
  106.4 71.7 reduce-scatter.4
  179.8 22.5 all-gather.6
  204.5 22.5 all-gather.8
  243.2 34.4 all-gather.10
  280.3 44.5 reduce-scatter.10
  327.4 44.5 reduce-scatter.8
  374.7 71.6 reduce-scatter.6
  451.6 145.2 all-reduce.101
where the time goes:
time: 622 us; the launch traced here: 611 us
  waiting for transfers between devices  316 us (51%)
  matrix products  89.1 us (14%)
  other arithmetic  71.1 us (11%)
  blocking collectives  66.6 us (11%)
  local copies, waits for them, and re-layouts  45.8 us (7%)
  between operations  18.1 us (3%)
    psum x1, waiting for transfers between devices, per_device(): lax.psum((mixer_grad, bias_part, out_grad, up_grad, down_grad), 'dp')  90.2 us
    reduce_scatter x1, waiting for transfers between devices, per_device(): lax.psum_scatter(matmul(lax.slice_in_dim(state_low, 0, local_tokens * lax...  67.3 us
    psum x1, blocking collectives, per_device(): lax.psum((gain_one_part, taps_part, gain_two_part), ('dp', 'tensor'))  44.7 us
    reduce_scatter x1, waiting for transfers between devices, per_device(): lax.psum_scatter(right_contract(lax.slice_in_dim(grad_proj_low, 0, local_...  37 us
    reduce_scatter x1, waiting for transfers between devices, per_device(): lax.psum_scatter(left_contract(normed_low, grad_up), 'tensor', scatter_di...  33.8 us
    all_gather x1, waiting for transfers between devices, per_device(): conv_full = lax.all_gather(conv_low, 'tensor', axis=0, tiled=True)  33.1 us
    unnamed x338, local copies, waits for them, and re-layouts  31.2 us
    dot_general x4, matrix products, left_contract(): lax.dot_general(left, right, (((0,), (0,)), ((), ())), preferred_element_...  28.3 us
  transfers between devices with their start and end apart: 11, of which 9 were waited for; matrix products, arithmetic and copies ran while one was open for 19% of the time, Pallas kernels for 0%

commit v1 on v0

v1 whole, which is shorter than its diff:
```python
import functools

import jax
import jax.numpy as jnp
from jax import lax
from jax.experimental import pallas as pl
from jax.experimental.pallas import tpu as pltpu
from jax.sharding import PartitionSpec as P

SHORT = 1024
LONG = 2048
VMEM_LIMIT = 63 * 1024 * 1024
epsilon = 1e-06
BF16 = jnp.bfloat16
F32 = jnp.float32


def rms_norm(values, gain):
    return values * lax.rsqrt(jnp.mean(values * values, axis=-1, keepdims=True) + epsilon) * gain


def contract(left, right, dims):
    return lax.dot_general(left, right, ((dims[:1], dims[1:]), ((), ())), preferred_element_type=F32)


def combine(before_pair, after_pair):
    return (before_pair[0] * after_pair[0], after_pair[0] * before_pair[1] + after_pair[1])


def row_facts(long_rows, short_rows, chunk):
    long_count, short_count = long_rows[0], short_rows[0]
    in_long = chunk < 2 * long_count
    in_row = chunk < 2 * long_count + short_count
    second = in_long & (chunk % 2 == 1)
    ends = in_row & (second | ~in_long)
    slot = jnp.where(in_long, chunk // 2, chunk - long_count)
    return in_row, second, ends, slot


def pair_swap(values, count):
    return lax.ppermute(values, "tensor", [(i, i ^ 1) for i in range(count)])


def plain(
    block_input, long_rows, short_rows, prev_states, norm1_gain, conv_weight, mixer_weight, gate_bias,
    out_weight, norm2_gain, up_weight, down_weight, cotangent,
):
    tokens, width = block_input.shape
    parts = lax.axis_size("tensor")
    me = lax.axis_index("tensor")
    rim = conv_weight.shape[0] - 1
    in_row, second, ends, slot = row_facts(long_rows, short_rows, me)
    mask = in_row.astype(F32)
    joined = second.astype(F32)
    even = (me % 2 == 0).astype(F32)
    slots = jnp.arange(prev_states.shape[0], dtype=jnp.int32)
    first_half = in_row & ~ends

    mixer_full = lax.all_gather(mixer_weight.astype(BF16), "tensor", axis=2, tiled=True)
    out_full = lax.all_gather(out_weight.astype(BF16), "tensor", axis=0, tiled=True)
    up_full = lax.all_gather(up_weight.astype(BF16), "tensor", axis=1, tiled=True)
    down_full = lax.all_gather(down_weight.astype(BF16), "tensor", axis=0, tiled=True)
    bias = lax.all_gather(gate_bias, "tensor", axis=0, tiled=True)
    prev = lax.all_gather(prev_states, "tensor", axis=1, tiled=True)
    start_state = jnp.sum(
        jnp.where((slots == slot)[:, None] & in_row & ~second, prev, 0.0), axis=0, keepdims=True
    )

    normed, norm1_back = jax.vjp(rms_norm, block_input, norm1_gain)
    rim_rows = pair_swap(normed[tokens - rim :], parts) * joined

    def convolve(extended, weight):
        total = weight[0] * extended[rim:]
        for tap in range(1, rim + 1):
            total = total + mask * weight[tap] * extended[rim - tap : rim - tap + tokens]
        return total

    conv_out, conv_back = jax.vjp(convolve, jnp.concatenate([rim_rows, normed], 0), conv_weight)
    conv_low = conv_out.astype(BF16)
    gate = contract(conv_low, mixer_full[0], (1, 0))
    cand = contract(conv_low, mixer_full[1], (1, 0))
    logit = gate + bias
    keep = jax.nn.sigmoid(-logit)
    opened = jax.nn.sigmoid(logit)
    soft = jax.nn.softplus(cand)
    factors, values = lax.associative_scan(combine, (keep, opened * soft), axis=0)
    ending = factors[-1:] * start_state + values[-1:]
    carry = start_state + joined * pair_swap(ending, parts)
    states = values + factors * carry
    before = jnp.concatenate([carry, states[:-1]], 0)
    end_table = jnp.where((slots == slot) & ends, 1.0, 0.0)[:, None]
    finals = lax.psum_scatter(end_table * states[-1:], "tensor", scatter_dimension=1, tiled=True)
    state_low = states.astype(BF16)
    mixed = contract(state_low, out_full, (1, 0))
    resid = block_input + mask * mixed
    normed_two, norm2_back = jax.vjp(rms_norm, resid, norm2_gain)
    normed_low = normed_two.astype(BF16)
    grad_branch = (mask * cotangent).astype(BF16)
    upward = contract(normed_low, up_full, (1, 0))
    activation, gelu_back = jax.vjp(lambda v: jax.nn.gelu(v, approximate=True), upward)
    activation_low = activation.astype(BF16)
    output = resid + mask * contract(activation_low, down_full, (1, 0))
    grad_act = contract(grad_branch, down_full, (1, 1))
    grad_up = gelu_back(grad_act)[0].astype(BF16)
    grad_norm_two = contract(grad_up, up_full, (1, 1))
    up_grad = contract(normed_low, grad_up, (0, 0))
    down_grad = contract(activation_low, grad_branch, (0, 0))
    grad_resid_norm, gain_two_part = norm2_back(grad_norm_two)
    grad_resid = cotangent + grad_resid_norm
    grad_mixed = (mask * grad_resid).astype(BF16)
    out_grad = contract(state_low, grad_mixed, (0, 0))
    grad_states = contract(grad_mixed, out_full, (1, 1))
    later_keep = jnp.concatenate([keep[1:], jnp.ones_like(keep[:1])], 0)
    back_factors, back_values = lax.associative_scan(combine, (later_keep, grad_states), axis=0, reverse=True)
    joins_next = (first_half & (me % 2 == 0)).astype(F32)
    back_carry = joins_next * pair_swap(keep[:1] * back_values[:1], parts)
    carried = back_values + back_factors * back_carry
    grad_logit = carried * (soft - before) * opened * (1 - opened)
    grad_cand = carried * opened * jax.nn.sigmoid(cand)
    bias_part = jnp.sum(grad_logit, axis=0)
    grad_logit_low = grad_logit.astype(BF16)
    grad_cand_low = grad_cand.astype(BF16)
    mixer_grad = jnp.stack([contract(conv_low, grad_logit_low, (0, 0)), contract(conv_low, grad_cand_low, (0, 0))])
    grad_conv = contract(grad_logit_low, mixer_full[0], (1, 1)) + contract(grad_cand_low, mixer_full[1], (1, 1))
    grad_extended, taps_part = conv_back(grad_conv)
    returned = joins_next * pair_swap(joined * grad_extended[:rim], parts)
    grad_normed = grad_extended[rim:] + jnp.concatenate(
        [jnp.zeros((tokens - rim, width), F32), returned], 0
    )
    grad_input_norm, gain_one_part = norm1_back(grad_normed)
    input_grad = grad_resid + grad_input_norm

    def scatter(grad, dim):
        return lax.psum_scatter(grad.astype(BF16), "tensor", scatter_dimension=dim, tiled=True)

    sharded = (
        scatter(mixer_grad, 2), scatter(out_grad, 0), scatter(up_grad, 1), scatter(down_grad, 0),
    )
    summed = tuple(g.astype(F32) for g in lax.psum(sharded, "dp"))
    shared = lax.psum((gain_one_part, taps_part, gain_two_part, bias_part), ("dp", "tensor"))
    channels = gate_bias.shape[0]
    bias_grad = lax.dynamic_slice_in_dim(shared[3], me * channels, channels)
    return (
        output, finals, input_grad, shared[0], shared[1], summed[0], bias_grad, summed[1], shared[2], summed[2], summed[3],
    )


LANES = 8
COLUMN = 128
MESH = pl.DeviceIdType.MESH
GELU_A = 0.7978845608028654
GELU_B = 0.044715


def dot(left, right, dims=(1, 0)):
    return lax.dot_general(left, right, ((dims[:1], dims[1:]), ((), ())), preferred_element_type=F32)


def rows_of(block, width):
    return block.reshape(-1, width)


class Wires:
    def __init__(self, send, recv):
        self.send, self.recv, self.used = send, recv, 0

    def copy(self, src, dst, device):
        k = self.used
        self.used += 1
        return pltpu.make_async_remote_copy(
            src_ref=src, dst_ref=dst, send_sem=self.send.at[k], recv_sem=self.recv.at[k],
            device_id=device, device_id_type=MESH,
        )


def count_wires(n, z_count, units):
    chips = n // 2
    gather = 4 * (1 + 4 * (chips - 1))
    unit = chips + (chips - 1) + 1 + 3 * (z_count - 1) + 1
    small = 1 + (chips - 1) + 1 + (z_count - 1)
    return gather + units * unit + small + 2 * (n - 1) + 2 + 1 + 2


def block_kernel(
    sizes, long_ref, short_ref, x_hbm, cot_hbm, lead_ref, gain1_ref, taps_ref, gain2_ref, mix_hbm, outw_hbm, up_hbm, down_hbm,
    output_hbm, igrad_hbm, finals_ref, small_ref, fin_up, fin_down, fin_out, fin_mix,
    xb, cb, n1h, res, gn2, fo, conv, t1, t2, n2, gm, act, gup, sig, st, ab, sp, sl,
    mix, outw, up, down,
    p_up, p_down, p_out,
    rc_up, ry_up, kx_up, rx_up, rz_up,
    rc_down, ry_down, kx_down, rx_down, rz_down,
    rc_out, ry_out, kx_out, rx_out, rz_out,
    ry_mix, kx_mix, rx_mix, rz_mix,
    lead, halo1, halo2, endrow, endin, tot, brow, bin_, fsend, frecv,
    acc_n1, acc_n2, acc_t, acc_b, pk, pk_core, pk_chip, pk_x, pk_z,
    send_sem, recv_sem, local_sem,
):
    n, z_count, tokens, width, hs, fs, slots, rim = sizes
    chips = n // 2
    steps = tokens // LANES
    columns = width // COLUMN
    tile = 256
    tiles = tokens // tile
    me = lax.axis_index("tensor")
    q, c = me // 2, me % 2
    dp = lax.axis_index("dp")
    z, x = dp // 2, dp % 2
    wires = Wires(send_sem, recv_sem)
    started = []

    def column(b):
        return pl.ds(b * COLUMN, COLUMN)

    def tensor(j):
        return (dp, j)

    sibling = tensor(me + 1 - 2 * c)
    partner = (dp + 1 - 2 * x, me)

    def z_peer(d):
        return ((((z + d) % z_count) * 2) + x, me)

    def shard_of(d, core):
        return ((q + d) % chips) * 2 + core

    def go(copy):
        copy.start()
        started.append(copy)
        return copy

    locals_ = [
        (mix_hbm.at[0], ab.at[0, pl.ds(0, width)]), (mix_hbm.at[1], ab.at[0, pl.ds(width, width)]),
        (outw_hbm, gn2.at[pl.ds(0, hs)]), (up_hbm, fo.at[pl.ds(0, width)]), (down_hbm, fo.at[pl.ds(width, fs)]),
    ]
    loads = [pltpu.make_async_copy(s, d, local_sem.at[i]) for i, (s, d) in enumerate(locals_)]
    x_loads = [pltpu.make_async_copy(x_hbm.at[:, column(b)], xb.at[b], local_sem.at[5 + b]) for b in range(columns)]
    cot_loads = [
        pltpu.make_async_copy(cot_hbm.at[:, column(b)], cb.at[b], local_sem.at[5 + columns + b]) for b in range(columns)
    ]
    for copy in loads[:3] + x_loads + loads[3:] + cot_loads:
        copy.start()

    barrier = pltpu.get_barrier_semaphore()
    peers = [tensor((me + d) % n) for d in range(1, n)] + [partner] + [z_peer(d) for d in range(1, z_count)]
    for peer in peers:
        pl.semaphore_signal(barrier, inc=1, device_id=peer, device_id_type=MESH)
    pl.semaphore_wait(barrier, len(peers))

    long_count, short_count = long_ref[0], short_ref[0]
    is_long = jnp.where(me < 2 * long_count, 1.0, 0.0)
    in_row = jnp.where(me < 2 * long_count + short_count, 1.0, 0.0)
    odd = (me % 2).astype(F32)
    joined = is_long * odd
    joins_next = is_long * (1.0 - odd)
    starts = in_row * (1.0 - joined)
    ends = in_row * (1.0 - joins_next)
    slot = jnp.where(me < 2 * long_count, me // 2, me - long_count)
    slot_mask = [jnp.where(slot == s, 1.0, 0.0) for s in range(slots)]

    gathers = {}

    def gather(name, ref):
        sib = go(wires.copy(ref.at[me], ref.at[me], sibling))
        far = [go(wires.copy(ref.at[me, x], ref.at[me, x], tensor(shard_of(d, c)))) for d in range(1, chips)]
        across, passed = [], []
        for d in range(1, chips):
            r = shard_of(chips - d, c)
            across.append(wires.copy(ref.at[r, x], ref.at[r, x], partner))
            passed.append((wires.copy(ref.at[r, x], ref.at[r, x], sibling), wires.copy(ref.at[r, 1 - x], ref.at[r, 1 - x], sibling)))
        gathers[name] = (sib, far, across, passed)

    def gather_far(name):
        _, far, across, passed = gathers[name]
        for d in range(chips - 1):
            far[d].wait_recv()
            go(across[d])
            go(passed[d][0])

    def gather_across(name):
        _, far, across, passed = gathers[name]
        for d in range(chips - 1):
            across[d].wait_recv()
            go(passed[d][1])

    def gather_passed(name):
        for one, two in gathers[name][3]:
            one.wait_recv()
            two.wait_recv()

    lead[me] = lead_ref[...]
    lead_copies = [go(wires.copy(lead.at[me], lead.at[me], tensor((me + d) % n))) for d in range(1, n)]
    loads[0].wait()
    loads[1].wait()
    half = width // 2
    for h in range(2):
        mix[me, h] = jnp.concatenate(
            [ab[0, pl.ds(h * half, half), :], ab[0, pl.ds(width + h * half, half), :]], axis=1
        ).astype(BF16)
    gather("mix", mix)
    loads[2].wait()
    outw[me] = gn2[pl.ds(0, hs), :].astype(BF16).reshape(2, hs // 2, width)

    def rest_of_weights():
        gather("out", outw)
        loads[3].wait()
        up[me] = fo[pl.ds(0, width), :].astype(BF16).reshape(up.shape[1:])
        gather("up", up)
        loads[4].wait()
        down[me] = fo[pl.ds(width, fs), :].astype(BF16).reshape(down.shape[1:])
        gather("down", down)

    rest_of_weights()

    def take(ref, i, count):
        return jnp.concatenate(
            [
                jnp.concatenate([ref[b, pl.ds(i * count + k, LANES, stride=steps), :] for b in range(columns)], axis=1)
                for k in range(count)
            ],
            axis=0,
        )

    def put(ref, i, count, value):
        for k in range(count):
            for b in range(columns):
                ref[b, pl.ds(i * count + k, LANES, stride=steps), :] = value[
                    k * LANES : (k + 1) * LANES, b * COLUMN : (b + 1) * COLUMN
                ]

    group = 4
    span = group * LANES
    spans = steps // group

    def at(i, shift=0, size=span):
        return pl.ds(pl.multiple_of(i * size + shift, LANES), size)

    def eights(value):
        return jnp.sum(value.reshape(-1, LANES, value.shape[-1]), axis=0)

    for copy in x_loads:
        copy.wait()
    gain1 = gain1_ref[...]
    gain2 = gain2_ref[...]

    @pl.loop(0, spans)
    def _(i):
        v = take(xb, i, group)
        scale = lax.rsqrt(jnp.mean(v * v, axis=-1, keepdims=True) + epsilon)
        n1h[at(i, rim * LANES), :] = v * scale * gain1
        res[at(i), :] = v

    edge = rim * LANES
    halo_copy = go(wires.copy(n1h.at[pl.ds(tokens, edge)], halo1, sibling))
    for copy in cot_loads:
        copy.wait()

    @pl.loop(0, spans)
    def _(i):
        gm[at(i), :] = (in_row * take(cb, i, group)).astype(BF16)

    halo_copy.wait_recv()
    sub = lax.broadcasted_iota(jnp.int32, (LANES, width), 0)
    for k in range(rim):
        own = pltpu.roll(n1h[pl.ds(tokens + k * LANES, LANES), :], 1, 0)
        other = pltpu.roll(halo1[pl.ds(k * LANES, LANES), :], 1, 0)
        n1h[pl.ds(k * LANES, LANES), :] = jnp.where(sub == 0, joined * other, own)
    tap = [taps_ref[pl.ds(k, 1), :] * (1.0 if k == 0 else in_row) for k in range(rim + 1)]

    @pl.loop(0, spans)
    def _(i):
        total = tap[0] * n1h[at(i, edge), :]
        for k in range(1, rim + 1):
            total = total + tap[k] * n1h[at(i, edge - k * LANES), :]
        conv[at(i), :] = total.astype(BF16)

    def project(j):
        weight = rows_of(mix[j], 2 * hs)
        bias = lead[j, pl.ds(slots, 1), :]

        @pl.loop(0, tiles)
        def _(t):
            rows = at(t, 0, tile)
            pre = dot(conv[rows, :], weight)
            logit = pre[:, :hs] + bias
            cand = pre[:, hs:]
            e = jnp.exp(-jnp.abs(logit))
            r = 1.0 / (1.0 + e)
            opened = jnp.where(logit >= 0, r, e * r)
            keep = jnp.where(logit >= 0, e * r, r)
            soft = jnp.maximum(cand, 0.0) + jnp.log1p(jnp.exp(-jnp.abs(cand)))
            sig[j, rows, :] = opened
            sp[j, rows, :] = soft
            ab[j, rows, :] = keep * in_row
            st[j, at(t, LANES, tile), :] = opened * soft

    for copy in lead_copies:
        copy.wait_recv()
    project(me)
    gathers["mix"][0].wait_recv()
    project(me + 1 - 2 * c)
    gather_far("mix")

    def transpose_to(dst, src):
        @pl.loop(0, tiles)
        def _(t):
            dst[:, pl.ds(pl.multiple_of(t * tile, tile), tile)] = src[at(t, 0, tile), :].T

    transpose_to(t2, gm)
    gather_far("out")
    gather_across("mix")
    for d in range(1, chips):
        project(shard_of(d, c))
    gather_across("out")
    gather_passed("mix")
    for d in range(1, chips):
        project(shard_of(d, 1 - c))
    gather_far("up")

    def scan_step(s, carry):
        rows = at(s, 0, LANES)
        later = at(s, LANES, LANES)
        out = []
        for j in range(n):
            fac, val = carry[j]
            a = ab[j, rows, :]
            b = st[j, later, :]
            fac = a * fac
            val = a * val + b
            ab[j, rows, :] = fac
            st[j, later, :] = val
            out.append((fac, val))
        return tuple(out)

    def unrolled(count, step, carry, by=4):
        def some(i, carry):
            for k in range(by):
                carry = step(i * by + k, carry)
            return carry

        return lax.fori_loop(0, count // by, some, carry)

    one = jnp.ones((LANES, hs), F32)
    zero = jnp.zeros((LANES, hs), F32)
    unrolled(steps, scan_step, tuple((one, zero) for _ in range(n)))
    last = pl.ds(tokens - LANES, LANES)

    def chain(j, carry, keep_rows):
        fac = ab[j, last, :]
        val = st[j, pl.ds(tokens, LANES), :]
        rows = []
        for g in range(LANES):
            rows.append(carry)
            carry = fac[g : g + 1] * carry + val[g : g + 1]
        if keep_rows:
            st[j, pl.ds(0, LANES), :] = jnp.concatenate(rows, axis=0)
        return carry

    first = []
    for j in range(n):
        begin = jnp.zeros((1, hs), F32)
        for s in range(slots):
            begin = begin + (starts * slot_mask[s]) * lead[j, pl.ds(s, 1), :]
        first.append(begin)
        endrow[j] = chain(j, begin, False)
    end_copy = go(wires.copy(endrow, endin, sibling))
    gather_across("up")
    gathers["out"][0].wait_recv()
    gather_passed("out")
    end_copy.wait_recv()
    for j in range(n):
        ending = chain(j, first[j] + joined * endin[j], True)
        for s in range(slots):
            fsend[j, pl.ds(s, 1), :] = (ends * slot_mask[s]) * ending
    final_copies = [
        go(wires.copy(fsend.at[(me + d) % n], frecv.at[d - 1], tensor((me + d) % n))) for d in range(1, n)
    ]

    @pl.loop(0, tiles)
    def _(t):
        rows = at(t, 0, tile)
        mixed = jnp.zeros((tile, width), F32)
        for j in range(n):
            into = st[j, pl.ds(0, LANES), :]
            value = st[j, at(t, LANES, tile), :] + (
                ab[j, rows, :].reshape(-1, LANES, hs) * into[None]
            ).reshape(tile, hs)
            st[j, at(t, LANES, tile), :] = value
            low = value.astype(BF16)
            sl[j, rows, :] = low
            mixed = mixed + dot(low, rows_of(outw[j], width))
        resid = res[rows, :] + in_row * mixed
        res[rows, :] = resid
        scale = lax.rsqrt(jnp.mean(resid * resid, axis=-1, keepdims=True) + epsilon)
        n2[rows, :] = (resid * scale * gain2).astype(BF16)

    gather_far("down")
    transpose_to(t1, n2)
    gather_passed("up")
    gather_across("down")
    gather_passed("down")
    gathers["up"][0].wait_recv()
    gathers["down"][0].wait_recv()

    sent_weights = list(started)

    class Sum:
        def __init__(self, part, rc, ry, kx, rx, rz, fin):
            self.part, self.rc, self.ry, self.kx, self.rx, self.rz, self.fin = part, rc, ry, kx, rx, rz, fin
            self.cols = part.shape[-1]
            self.piece = part.shape[-2]
            self.c1 = [None] * chips
            self.c1_wires = [wires.used + i for i in range(chips)]
            wires.used += chips

        def one(self, d):
            k = (q + d) % chips
            copy = pltpu.make_async_remote_copy(
                src_ref=self.part.at[shard_of(d, 1 - c)], dst_ref=self.rc.at[d], send_sem=send_sem.at[self.c1_wires[d]],
                recv_sem=recv_sem.at[self.c1_wires[d]], device_id=sibling, device_id_type=MESH,
            )
            self.c1[d] = go(copy)

        def two(self):
            self.c2 = []
            for d in range(1, chips):
                self.c1[d].wait_recv()
                j = shard_of(d, c)

                @pl.loop(0, 2)
                def _(h, j=j, d=d):
                    self.part[j, h] = (self.part[j, h].astype(F32) + self.rc[d, h].astype(F32)).astype(BF16)

                self.c2.append(go(wires.copy(self.part.at[j], self.ry.at[d - 1], tensor(j))))

        def total(self, h):
            v = self.part[me, h].astype(F32) + self.rc[0, h].astype(F32)
            for d in range(chips - 1):
                v = v + self.ry[d, h].astype(F32)
            return v

        def three(self):
            self.c1[0].wait_recv()
            for copy in self.c2:
                copy.wait_recv()
            self.part[me, 1 - x] = self.total(1 - x).astype(BF16)
            self.c3 = go(wires.copy(self.part.at[me, 1 - x], self.rx, partner))
            self.kx[...] = self.total(x)

        def four(self):
            self.c3.wait_recv()
            v = self.kx[...] + self.rx[...].astype(F32)
            self.kx[...] = v
            self.part[me, x] = v.astype(BF16)
            self.c4 = [
                go(wires.copy(self.part.at[me, x, (z + d) % z_count], self.rz.at[d - 1], z_peer(d))) for d in range(1, z_count)
            ]

        def five(self):
            for copy in self.c4:
                copy.wait_recv()
            v = self.kx[z]
            for d in range(z_count - 1):
                v = v + self.rz[d].astype(F32)
            self.fin[x, z] = v.astype(BF16)
            mine = self.fin.at[x, z]
            self.c5 = [go(wires.copy(mine, mine, z_peer(d))) for d in range(1, z_count)]
            self.c6 = [go(wires.copy(mine, mine, partner))]

        def six(self):
            for d in range(1, z_count):
                self.c5[d - 1].wait_recv()
                theirs = self.fin.at[x, (z + z_count - d) % z_count]
                self.c6.append(go(wires.copy(theirs, theirs, partner)))

        def end(self):
            for copy in self.c6:
                copy.wait_recv()

    s_up = Sum(p_up, rc_up, ry_up, kx_up, rx_up, rz_up, fin_up)
    s_down = Sum(p_down, rc_down, ry_down, kx_down, rx_down, rz_down, fin_down)
    s_out = Sum(p_out, rc_out, ry_out, kx_out, rx_out, rz_out, fin_out)
    s_mix = Sum(up, down, ry_mix, kx_mix, rx_mix, rz_mix, fin_mix)

    def weight_grad(unit, j, left, right, cols):
        step = 256
        for k in range(cols // step):
            value = dot(left[...], right(pl.ds(k * step, step)))
            unit.part[j, :, :, :, pl.ds(k * step, step)] = value.astype(BF16).reshape(unit.part.shape[1:-1] + (step,))

    def feed(j, begin):
        @pl.loop(0, tiles)
        def _(t):
            rows = at(t, 0, tile)
            upw = rows_of(up[j], fs)
            downw = rows_of(down[j], width)
            u = dot(n2[rows, :], upw)
            ga = dot(gm[rows, :], downw, (1, 1))
            u2 = u * u
            th = jnp.tanh(GELU_A * u * (1.0 + GELU_B * u2))
            hp = 0.5 + 0.5 * th
            a = (u * hp).astype(BF16)
            slope = hp + (0.5 * GELU_A) * u * (1.0 - th * th) * (1.0 + 3.0 * GELU_B * u2)
            gu = (ga * slope).astype(BF16)
            act[rows, :] = a
            gup[rows, :] = gu
            o = dot(a, downw)
            g = dot(gu, upw, (1, 1))
            if begin:
                fo[rows, :] = o
                gn2[rows, :] = g
            else:
                fo[rows, :] = fo[rows, :] + o
                gn2[rows, :] = gn2[rows, :] + g

        weight_grad(s_up, j, t1, lambda k: gup[:, k], fs)
        weight_grad(s_down, j, t2, lambda k: act[:, k], fs)

    for d in range(1, chips):
        feed(shard_of(d, 1 - c), d == 1)
        s_up.one(d)
        s_down.one(d)
        feed(shard_of(d, c), False)
    s_up.two()
    s_down.two()
    feed(me + 1 - 2 * c, False)
    s_up.one(0)
    s_down.one(0)
    feed(me, False)

    acc_n2[...] = jnp.zeros_like(acc_n2)

    @pl.loop(0, spans)
    def _(i):
        r = res[at(i), :]
        g = gn2[at(i), :]
        scale = lax.rsqrt(jnp.mean(r * r, axis=-1, keepdims=True) + epsilon)
        gg = g * gain2
        m = jnp.mean(gg * r, axis=-1, keepdims=True)
        gr = take(cb, i, group) + scale * gg - r * (scale * scale * scale * m)
        acc_n2[...] += eights(g * r * scale)
        gn2[at(i), :] = gr
        gm[at(i), :] = (in_row * gr).astype(BF16)
        put(cb, i, group, r + in_row * fo[at(i), :])

    def store(ref, hbm):
        copies = [
            pltpu.make_async_copy(ref.at[b], hbm.at[:, column(b)], local_sem.at[next_local[0] + b]) for b in range(columns)
        ]
        next_local[0] += columns
        for copy in copies:
            copy.start()
        return copies

    next_local = [5 + 2 * columns]
    stores = store(cb, output_hbm)
    for copy in sent_weights:
        copy.wait_send()
        started.remove(copy)
    s_up.three()

    transpose_to(t2, gm)
    for d in list(range(1, chips)) + [0]:
        for core in (1 - c, c):
            j = shard_of(d, core)
            weight_grad(s_out, j, t2, lambda k, j=j: sl[j, :, k], hs)
        s_out.one(d)
    s_down.three()
    transpose_to(t1, conv)
    s_out.two()
    s_up.four()

    for j in range(n):
        acc_b[j] = jnp.zeros((LANES, hs), F32)

    def recur_back(d, begin, between):
        js = [shard_of(d, core) for core in range(2)]
        for k in range(2):
            j = js[k]

            @pl.loop(0, tiles)
            def _(t, j=j, k=k):
                ab[k, at(t, 0, tile), :] = dot(gm[at(t, 0, tile), :], rows_of(outw[j], width), (1, 1))

        def back_step(i, carry):
            s = steps - 1 - i
            rows = at(s, 0, LANES)
            out = []
            for k in range(2):
                fac, val, keep = carry[k]
                fac = keep * fac
                val = ab[k, rows, :] + keep * val
                ab[2 + k, rows, :] = fac
                ab[k, rows, :] = val
                out.append((fac, val, 1.0 - sig[js[k], rows, :]))
            return tuple(out)

        unrolled(steps, back_step, ((one, zero, one), (one, zero, one)))

        def chain_back(k, carry):
            fac = ab[2 + k, pl.ds(0, LANES), :]
            val = ab[k, pl.ds(0, LANES), :]
            keep = 1.0 - sig[js[k], pl.ds(0, LANES), :]
            rows = []
            for g in reversed(range(LANES)):
                rows.append(carry)
                carry = keep[g : g + 1] * (val[g : g + 1] + fac[g : g + 1] * carry)
            return carry, jnp.concatenate(rows[::-1], axis=0)

        slot_ = 2 * d
        for k in range(2):
            brow[slot_ + k] = chain_back(k, jnp.zeros((1, hs), F32))[0]
        copy = go(wires.copy(brow.at[pl.ds(slot_, 2)], bin_.at[pl.ds(slot_, 2)], sibling))
        between()
        copy.wait_recv()
        for k in (0, 1):
            j = js[k]
            into = chain_back(k, joins_next * bin_[slot_ + k])[1]
            weight = rows_of(mix[j], 2 * hs)

            @pl.loop(0, tiles)
            def _(t, j=j, k=k, into=into, weight=weight):
                rows = at(t, 0, tile)
                carried = ab[k, rows, :] + (ab[2 + k, rows, :].reshape(-1, LANES, hs) * into[None]).reshape(tile, hs)
                opened = sig[j, rows, :]
                soft = sp[j, rows, :]
                weighted = carried * opened
                gl = weighted * (soft - st[j, rows, :]) * (1.0 - opened)
                close = jnp.where(soft < 0.01, soft * (1.0 - soft * (0.5 - soft * (1.0 / 6.0))), 1.0 - jnp.exp(-soft))
                gc = weighted * close
                acc_b[j] += eights(gl)
                gp = jnp.concatenate([gl.astype(BF16), gc.astype(BF16)], axis=1)
                act[rows, :] = gp
                back = dot(gp, weight, (1, 1))
                if begin and k == 0:
                    res[rows, :] = back
                else:
                    res[rows, :] = res[rows, :] + back

            weight_grad(s_mix, j, t1, lambda kk: act[:, kk], 2 * hs)

    def after_first():
        s_down.four()

    for d in range(1, chips):
        recur_back(d, d == 1, after_first if d == 1 else (lambda: None))
        s_mix.one(d)
    s_up.five()

    def between_last():
        s_mix.two()
        s_out.three()

    recur_back(0, chips == 1, between_last)
    s_mix.one(0)
    halo_back = go(wires.copy(res.at[pl.ds(0, edge)], halo2, sibling))
    s_down.five()
    s_up.six()
    s_out.four()
    s_mix.three()

    halo_back.wait_recv()
    for k in range(rim):
        own = pltpu.roll(res[pl.ds(k * LANES, LANES), :], LANES - 1, 0)
        other = pltpu.roll(halo2[pl.ds(k * LANES, LANES), :], LANES - 1, 0)
        res[pl.ds(tokens + k * LANES, LANES), :] = jnp.where(sub == LANES - 1, joins_next * other, own)
    acc_n1[...] = jnp.zeros_like(acc_n1)
    acc_t[...] = jnp.zeros_like(acc_t)

    def norm1_back(i):
        g0 = res[at(i), :]
        total = tap[0] * g0
        acc_t[0] += eights(g0 * n1h[at(i, edge), :])
        for k in range(1, rim + 1):
            total = total + tap[k] * res[at(i, k * LANES), :]
            acc_t[k] += eights(g0 * n1h[at(i, edge - k * LANES), :])
        v = take(xb, i, group)
        scale = lax.rsqrt(jnp.mean(v * v, axis=-1, keepdims=True) + epsilon)
        gg = total * gain1
        m = jnp.mean(gg * v, axis=-1, keepdims=True)
        acc_n1[...] += eights(total * v * scale)
        put(xb, i, group, gn2[at(i), :] + scale * gg - v * (scale * scale * scale * m))

    pl.loop(0, spans)(norm1_back)
    stores += store(xb, igrad_hbm)

    pk[...] = jnp.zeros_like(pk)
    pk[pl.ds(0, 1), :] = jnp.sum(acc_n1[...], axis=0, keepdims=True)
    for k in range(rim + 1):
        pk[pl.ds(1 + k, 1), :] = jnp.sum(acc_t[k], axis=0, keepdims=True)
    pk[pl.ds(6, 1), :] = jnp.sum(acc_n2[...], axis=0, keepdims=True)
    for j in range(n):
        pk[pl.ds(8 + j, 1), pl.ds(0, hs)] = jnp.sum(acc_b[j], axis=0, keepdims=True)
    k1 = go(wires.copy(pk, pk_core, sibling))
    s_mix.four()
    s_out.five()
    k1.wait_recv()
    pk_chip[q] = pk[...] + pk_core[...]
    k2 = [go(wires.copy(pk_chip.at[q], pk_chip.at[q], tensor(shard_of(d, c)))) for d in range(1, chips)]
    s_down.six()
    for copy in k2:
        copy.wait_recv()
    value = pk_chip[0]
    for k in range(1, chips):
        value = value + pk_chip[k]
    pk_x[0] = value
    k3 = go(wires.copy(pk_x.at[0], pk_x.at[1], partner))
    s_mix.five()
    s_out.six()
    k3.wait_recv()
    pk_z[z] = pk_x[0] + pk_x[1]
    k4 = [go(wires.copy(pk_z.at[z], pk_z.at[z], z_peer(d))) for d in range(1, z_count)]
    s_mix.six()
    for copy in final_copies:
        copy.wait_recv()
    total = fsend[me]
    for d in range(n - 1):
        total = total + frecv[d]
    finals_ref[...] = total
    for copy in k4:
        copy.wait_recv()
    value = pk_z[0]
    for k in range(1, z_count):
        value = value + pk_z[k]
    small_ref[...] = value
    for unit in (s_up, s_down, s_out, s_mix):
        unit.end()
    for copy in started:
        copy.wait_send()
    for copy in stores:
        copy.wait()


def fused(
    block_input, long_rows, short_rows, prev_states, norm1_gain, conv_weight, mixer_weight, gate_bias,
    out_weight, norm2_gain, up_weight, down_weight, cotangent,
):
    tokens, width = block_input.shape
    n = lax.axis_size("tensor")
    z_count = lax.axis_size("dp") // 2
    chips = n // 2
    slots, hs = prev_states.shape
    fs = up_weight.shape[1]
    rim = conv_weight.shape[0] - 1
    steps = tokens // LANES
    piece = width // (2 * z_count)
    lead_in = jnp.concatenate([prev_states, gate_bias[None]], axis=0)
    pk_rows = 8 + -(-n // 8) * 8
    units = [fs, fs, hs, 2 * hs]

    def full(cols):
        return pltpu.VMEM((n, 2, z_count, piece, cols), BF16)

    def sums(cols):
        return [
            pltpu.VMEM((chips, 2, z_count, piece, cols), BF16),
            pltpu.VMEM((max(chips - 1, 1), 2, z_count, piece, cols), BF16),
            pltpu.VMEM((z_count, piece, cols), F32),
            pltpu.VMEM((z_count, piece, cols), BF16),
            pltpu.VMEM((max(z_count - 1, 1), piece, cols), BF16),
        ]

    def wide(rows, kind=F32):
        return pltpu.VMEM((rows, width), kind)

    by_column = pltpu.VMEM((width // COLUMN, tokens, COLUMN), F32)
    per_block = pltpu.VMEM((n, tokens, hs), F32)
    scratch = [
        by_column, by_column, wide(tokens + rim * LANES), wide(tokens + rim * LANES), wide(tokens), wide(tokens),
        wide(tokens, BF16), pltpu.VMEM((width, tokens), BF16), pltpu.VMEM((width, tokens), BF16), wide(tokens, BF16),
        wide(tokens, BF16), pltpu.VMEM((tokens, fs), BF16), pltpu.VMEM((tokens, fs), BF16),
        per_block, pltpu.VMEM((n, tokens + LANES, hs), F32), per_block, per_block, pltpu.VMEM((n, tokens, hs), BF16),
        pltpu.VMEM((n, 2, width // 2, 2 * hs), BF16), pltpu.VMEM((n, 2, hs // 2, width), BF16), full(fs),
        full(fs),
        full(fs), full(fs), full(hs),
        *sums(fs), *sums(fs), *sums(hs), *sums(2 * hs)[1:],
        pltpu.VMEM((n, slots + 1, hs), F32), wide(rim * LANES), wide(rim * LANES), pltpu.VMEM((n, 1, hs), F32),
        pltpu.VMEM((n, 1, hs), F32), pltpu.VMEM((8, 128), F32), pltpu.VMEM((n, 1, hs), F32), pltpu.VMEM((n, 1, hs), F32),
        pltpu.VMEM((n, slots, hs), F32), pltpu.VMEM((n - 1, slots, hs), F32),
        wide(LANES), wide(LANES), pltpu.VMEM((rim + 1, LANES, width), F32), pltpu.VMEM((n, LANES, hs), F32),
        wide(pk_rows), wide(pk_rows), pltpu.VMEM((chips, pk_rows, width), F32), pltpu.VMEM((2, pk_rows, width), F32),
        pltpu.VMEM((z_count, pk_rows, width), F32),
    ]
    wire_count = count_wires(n, z_count, 4)
    scratch += [
        pltpu.SemaphoreType.DMA((wire_count,)), pltpu.SemaphoreType.DMA((wire_count,)), pltpu.SemaphoreType.DMA((5 + 4 * (width // COLUMN),)),
    ]
    vmem = pl.BlockSpec(memory_space=pltpu.VMEM)
    smem = pl.BlockSpec(memory_space=pltpu.SMEM)
    hbm = pl.BlockSpec(memory_space=pl.ANY)

    def shape(dims, kind=F32):
        return jax.ShapeDtypeStruct(dims, kind)

    outs = pl.pallas_call(
        functools.partial(block_kernel, (n, z_count, tokens, width, hs, fs, slots, rim)),
        out_shape=[
            shape((tokens, width)), shape((tokens, width)), shape((slots, hs)), shape((pk_rows, width)),
            *[shape((2, z_count, piece, cols), BF16) for cols in units],
        ],
        in_specs=[smem, smem, hbm, hbm, vmem, vmem, vmem, vmem, hbm, hbm, hbm, hbm],
        out_specs=[hbm, hbm] + [vmem] * 6,
        scratch_shapes=scratch,
        compiler_params=pltpu.CompilerParams(collective_id=0, has_side_effects=True, vmem_limit_bytes=VMEM_LIMIT),
    )(
        long_rows, short_rows, block_input, cotangent, lead_in, norm1_gain[None], conv_weight, norm2_gain[None],
        mixer_weight, out_weight, up_weight, down_weight,
    )
    output, input_grad, finals, small, g_up, g_down, g_out, g_mix = outs
    me = lax.axis_index("tensor")
    g_up, g_down, g_out, g_mix = (g.reshape(width, -1).astype(F32) for g in (g_up, g_down, g_out, g_mix))
    mixer_grad = jnp.stack([g_mix[:, :hs], g_mix[:, hs:]])
    bias_grad = lax.dynamic_slice(small, (8 + me, 0), (1, hs))[0]
    return (
        output, finals, input_grad, small[0], small[1 : 2 + rim], mixer_grad, bias_grad, g_out.T, small[6], g_up, g_down.T,
    )


def solution(mesh):
    takes_kernel = mesh.shape["tensor"] == 4 and mesh.shape["dp"] % 2 == 0
    rows = P(("dp", "tensor"), None)
    placed = (
        rows, P("dp"), P("dp"), P("dp", "tensor"), P(), P(), P(None, None, "tensor"), P("tensor"),
        P("tensor", None), P(), P(None, "tensor"), P("tensor", None), rows,
    )
    return jax.shard_map(
        fused if takes_kernel else plain,
        mesh=mesh,
        in_specs=placed,
        out_specs=(
            rows, P("dp", "tensor"), rows, P(), P(), P(None, None, "tensor"), P("tensor"), P("tensor", None),
            P(), P(None, "tensor"), P("tensor", None),
        ),
        check_vma=False,
    )
```

time: 622 us -> 157 us (0.25); the launches traced: 611 us -> 156 us
  waiting for transfers between devices: 316 us -> 0 us
  Pallas kernels: 0 us -> 139 us
  matrix products: 89.1 us -> 0 us
  blocking collectives: 66.6 us -> 0 us
  other arithmetic: 71.1 us -> 4.82 us
  local copies, waits for them, and re-layouts: 45.8 us -> 10.5 us
  between operations: 18.1 us -> 2 us
    pallas_call x0 -> x1, Pallas kernels: none -> 139 us  [fused(): pl.pallas_call(functools.partial(block_kernel, (n, z_count, tokens, width...]
    reduce_scatter x4 -> x0, waiting for transfers between devices: 138 us -> none  [the longest x1 67.3 us: per_device(): lax.psum_scatter(matmul(lax.slice_in_dim(state_low, 0, local_tokens * lax...]
    psum x1 -> x0, waiting for transfers between devices: 90.2 us -> none  [per_device(): lax.psum((mixer_grad, bias_part, out_grad, up_grad, down_grad), 'dp')]
    dot_general x14 -> x0, matrix products: 89.1 us -> none  [the longest x4 28.3 us: left_contract(): lax.dot_general(left, right, (((0,), (0,)), ((), ())), preferred_element_...]
    all_gather x4 -> x0, waiting for transfers between devices: 87.2 us -> none  [the longest x1 33.1 us: per_device(): conv_full = lax.all_gather(conv_low, 'tensor', axis=0, tiled=True)]
    psum x2 -> x0, blocking collectives: 66.6 us -> none  [the longest x1 44.7 us: per_device(): lax.psum((gain_one_part, taps_part, gain_two_part), ('dp', 'tensor'))]
    unnamed x338 -> x15, local copies, waits for them, and re-layouts: 31.2 us -> 4.08 us
    reduce_sum x6 -> x0, other arithmetic: 24.7 us -> none  [the longest x1 10.6 us: recurrence(): logit = projected[:, :channels] + bias]
  transfers between devices with their start and end apart: 11 -> 0, of which waited for: 9 -> 0; matrix products, arithmetic and copies ran while one was open for 19% -> 0% of each run, Pallas kernels for 0% -> 0%
where the time goes in v1:
time: 157 us; the launch traced here: 156 us
  Pallas kernels  139 us (89%)
  local copies, waits for them, and re-layouts  10.5 us (7%)
  other arithmetic  4.82 us (3%)
  between operations  2 us (1%)
    pallas_call x1, Pallas kernels, fused(): pl.pallas_call(functools.partial(block_kernel, (n, z_count, tokens, width...  139 us
    unnamed x15, local copies, waits for them, and re-layouts  4.08 us

profile of v1, /device:TPU:0, one launch (start us, length us, event | category | flops | bytes accessed | tf_op | source)
XLA Modules:
  0.0 155.9 jit_solution(7802480757489719108)
XLA Ops:
  1.9 1.3 pad_maximum_fusion.1.lead_ref
  3.2 138.6 %shard_map.212 = (f32[1024,512]{1,0:T(8,128)}, f32[1024,512]{1,0:T(8,128)}, f32[4,256]{1,0:T(4,128)}, f32[16,512]{1,0:T(8,128)}, bf16[2,4,64,512]{3,2,1,0:T(8,12...) custom-call(s32[1]{0:T(128)S(6)} %copy.29.long_ref, ...), custom_call_target="tpu_custom_call" | custom-call | tf_op jit(solution)/shard_map/pallas_call | solution.py:894
  141.9 0.0 copy-start.2
  141.9 1.3 constant_dynamic-slice_fusion
  143.2 1.4 fusion
  144.6 1.3 slice.16
  145.9 1.0 bitcast_convert_fusion.3
  146.9 1.0 copy.24
  147.9 0.0 copy-done.2
  147.9 0.2 bitcast_convert_fusion.2
  148.0 0.0 copy-start.3
  148.0 0.0 copy-start.4
  148.1 0.1 slice_bitcast_fusion.1
  148.1 1.0 pad_maximum_fusion
  149.2 0.0 copy-done.3
  149.2 0.4 copy-done.4
  149.6 0.0 copy-start.1
  149.6 1.3 bitcast_convert_fusion
  150.9 1.3 copy.25
  152.2 0.0 copy-done.1
  152.2 0.0 copy-start.5
  152.2 0.0 copy-start
  152.2 1.3 copy.31
  153.5 0.0 copy-done.5
  153.5 0.6 copy.32
  154.1 0.4 copy-done
  154.6 1.3 copy.33
Async XLA Ops:
  141.9 6.0 %copy-start.2 = (bf16[2,4,64,512]{3,2,1,0:T(8,128)(2,1)S(1)}, bf16[2,4,64,512]{3,2,1,0:T(8,128)(2,1)}, u32[]{:S(2)}) copy-start(bf16[2,4,64,512]{3,2,1,0:T(8,128)(2,1)} %get-tuple-element.23) | copy-start | bytes 1572868
  148.0 1.1 copy-start.3
  148.0 1.5 copy-start.4
  149.6 2.6 %copy-start.1 = (f32[1024,512]{1,0:T(8,128)S(1)}, f32[1024,512]{1,0:T(8,128)}, u32[]{:S(2)}) copy-start(f32[1024,512]{1,0:T(8,128)} %get-tuple-element.44) | copy-start | bytes 6291460
  152.2 1.3 copy-start.5
  152.2 2.4 %copy-start = (f32[1024,512]{1,0:T(8,128)S(1)}, f32[1024,512]{1,0:T(8,128)}, u32[]{:S(2)}) copy-start(f32[1024,512]{1,0:T(8,128)} %get-tuple-element.46) | copy-start | bytes 6291460

commit v2 on v1

v2 whole, which is shorter than its diff:
```python
import functools

import jax
import jax.numpy as jnp
from jax import lax
from jax.experimental import pallas as pl
from jax.experimental.pallas import tpu as pltpu
from jax.sharding import PartitionSpec as P

SHORT = 1024
LONG = 2048
VMEM_LIMIT = 63 * 1024 * 1024
epsilon = 1e-06
BF16 = jnp.bfloat16
F32 = jnp.float32


def rms_norm(values, gain):
    return values * lax.rsqrt(jnp.mean(values * values, axis=-1, keepdims=True) + epsilon) * gain


def contract(left, right, dims):
    return lax.dot_general(left, right, ((dims[:1], dims[1:]), ((), ())), preferred_element_type=F32)


def combine(before_pair, after_pair):
    return (before_pair[0] * after_pair[0], after_pair[0] * before_pair[1] + after_pair[1])


def row_facts(long_rows, short_rows, chunk):
    long_count, short_count = long_rows[0], short_rows[0]
    in_long = chunk < 2 * long_count
    in_row = chunk < 2 * long_count + short_count
    second = in_long & (chunk % 2 == 1)
    ends = in_row & (second | ~in_long)
    slot = jnp.where(in_long, chunk // 2, chunk - long_count)
    return in_row, second, ends, slot


def pair_swap(values, count):
    return lax.ppermute(values, "tensor", [(i, i ^ 1) for i in range(count)])


def plain(
    block_input, long_rows, short_rows, prev_states, norm1_gain, conv_weight, mixer_weight, gate_bias,
    out_weight, norm2_gain, up_weight, down_weight, cotangent,
):
    tokens, width = block_input.shape
    parts = lax.axis_size("tensor")
    me = lax.axis_index("tensor")
    rim = conv_weight.shape[0] - 1
    in_row, second, ends, slot = row_facts(long_rows, short_rows, me)
    mask = in_row.astype(F32)
    joined = second.astype(F32)
    even = (me % 2 == 0).astype(F32)
    slots = jnp.arange(prev_states.shape[0], dtype=jnp.int32)
    first_half = in_row & ~ends

    mixer_full = lax.all_gather(mixer_weight.astype(BF16), "tensor", axis=2, tiled=True)
    out_full = lax.all_gather(out_weight.astype(BF16), "tensor", axis=0, tiled=True)
    up_full = lax.all_gather(up_weight.astype(BF16), "tensor", axis=1, tiled=True)
    down_full = lax.all_gather(down_weight.astype(BF16), "tensor", axis=0, tiled=True)
    bias = lax.all_gather(gate_bias, "tensor", axis=0, tiled=True)
    prev = lax.all_gather(prev_states, "tensor", axis=1, tiled=True)
    start_state = jnp.sum(
        jnp.where((slots == slot)[:, None] & in_row & ~second, prev, 0.0), axis=0, keepdims=True
    )

    normed, norm1_back = jax.vjp(rms_norm, block_input, norm1_gain)
    rim_rows = pair_swap(normed[tokens - rim :], parts) * joined

    def convolve(extended, weight):
        total = weight[0] * extended[rim:]
        for tap in range(1, rim + 1):
            total = total + mask * weight[tap] * extended[rim - tap : rim - tap + tokens]
        return total

    conv_out, conv_back = jax.vjp(convolve, jnp.concatenate([rim_rows, normed], 0), conv_weight)
    conv_low = conv_out.astype(BF16)
    gate = contract(conv_low, mixer_full[0], (1, 0))
    cand = contract(conv_low, mixer_full[1], (1, 0))
    logit = gate + bias
    keep = jax.nn.sigmoid(-logit)
    opened = jax.nn.sigmoid(logit)
    soft = jax.nn.softplus(cand)
    factors, values = lax.associative_scan(combine, (keep, opened * soft), axis=0)
    ending = factors[-1:] * start_state + values[-1:]
    carry = start_state + joined * pair_swap(ending, parts)
    states = values + factors * carry
    before = jnp.concatenate([carry, states[:-1]], 0)
    end_table = jnp.where((slots == slot) & ends, 1.0, 0.0)[:, None]
    finals = lax.psum_scatter(end_table * states[-1:], "tensor", scatter_dimension=1, tiled=True)
    state_low = states.astype(BF16)
    mixed = contract(state_low, out_full, (1, 0))
    resid = block_input + mask * mixed
    normed_two, norm2_back = jax.vjp(rms_norm, resid, norm2_gain)
    normed_low = normed_two.astype(BF16)
    grad_branch = (mask * cotangent).astype(BF16)
    upward = contract(normed_low, up_full, (1, 0))
    activation, gelu_back = jax.vjp(lambda v: jax.nn.gelu(v, approximate=True), upward)
    activation_low = activation.astype(BF16)
    output = resid + mask * contract(activation_low, down_full, (1, 0))
    grad_act = contract(grad_branch, down_full, (1, 1))
    grad_up = gelu_back(grad_act)[0].astype(BF16)
    grad_norm_two = contract(grad_up, up_full, (1, 1))
    up_grad = contract(normed_low, grad_up, (0, 0))
    down_grad = contract(activation_low, grad_branch, (0, 0))
    grad_resid_norm, gain_two_part = norm2_back(grad_norm_two)
    grad_resid = cotangent + grad_resid_norm
    grad_mixed = (mask * grad_resid).astype(BF16)
    out_grad = contract(state_low, grad_mixed, (0, 0))
    grad_states = contract(grad_mixed, out_full, (1, 1))
    later_keep = jnp.concatenate([keep[1:], jnp.ones_like(keep[:1])], 0)
    back_factors, back_values = lax.associative_scan(combine, (later_keep, grad_states), axis=0, reverse=True)
    joins_next = (first_half & (me % 2 == 0)).astype(F32)
    back_carry = joins_next * pair_swap(keep[:1] * back_values[:1], parts)
    carried = back_values + back_factors * back_carry
    grad_logit = carried * (soft - before) * opened * (1 - opened)
    grad_cand = carried * opened * jax.nn.sigmoid(cand)
    bias_part = jnp.sum(grad_logit, axis=0)
    grad_logit_low = grad_logit.astype(BF16)
    grad_cand_low = grad_cand.astype(BF16)
    mixer_grad = jnp.stack([contract(conv_low, grad_logit_low, (0, 0)), contract(conv_low, grad_cand_low, (0, 0))])
    grad_conv = contract(grad_logit_low, mixer_full[0], (1, 1)) + contract(grad_cand_low, mixer_full[1], (1, 1))
    grad_extended, taps_part = conv_back(grad_conv)
    returned = joins_next * pair_swap(joined * grad_extended[:rim], parts)
    grad_normed = grad_extended[rim:] + jnp.concatenate(
        [jnp.zeros((tokens - rim, width), F32), returned], 0
    )
    grad_input_norm, gain_one_part = norm1_back(grad_normed)
    input_grad = grad_resid + grad_input_norm

    def scatter(grad, dim):
        return lax.psum_scatter(grad.astype(BF16), "tensor", scatter_dimension=dim, tiled=True)

    sharded = (
        scatter(mixer_grad, 2), scatter(out_grad, 0), scatter(up_grad, 1), scatter(down_grad, 0),
    )
    summed = tuple(g.astype(F32) for g in lax.psum(sharded, "dp"))
    shared = lax.psum((gain_one_part, taps_part, gain_two_part, bias_part), ("dp", "tensor"))
    channels = gate_bias.shape[0]
    bias_grad = lax.dynamic_slice_in_dim(shared[3], me * channels, channels)
    return (
        output, finals, input_grad, shared[0], shared[1], summed[0], bias_grad, summed[1], shared[2], summed[2], summed[3],
    )


LANES = 8
MESH = pl.DeviceIdType.MESH
CHUNKS = (2, 2, 1, 4)
WIRES = 256
SCHEDULE = {
    "own": (("g", "mix", "far", 0),),
    "gm": (("g", "mix", "far", 1),),
    "mixfar!": (("g", "out", "far", 0), ("g", "mix", "across", 0), ("g", "up", "far", 0), ("g", "mix", "across", 1)),
    "scan2": (("g", "out", "across", 0), ("g", "up", "far", 1)),
    "end!": (("g", "down", "far", 0), ("g", "up", "across", 0)),
    "states": (("g", "down", "far", 1), ("g", "up", "across", 1)),
    "updown!": (("g", "down", "across", 0), ("g", "down", "across", 1)),
    "f2a": (("up", "y", 0), ("up", "y", 1), ("down", "xa", 1, 0), ("down", "xa", 1, 1)),
    "f3b": (("down", "ya", 0),),
    "f3d": (("down", "ya", 1),),
    "B1a": (("up", "x", 0), ("down", "xa", 0, 0), ("down", "xa", 0, 1)),
    "r1g": (("up", "x", 1),),
    "r1w!": (("out", "y", 0), ("up", "z", 0)),
    "r1w0": (("down", "z", 0),),
    "r0g": (("up", "zb", 0), ("down", "z", 1)),
    "r0w!": (("up", "z", 1), ("mix", "y", 0), ("mix", "y", 1), ("mix", "y", 2), ("mix", "y", 3), ("down", "zb", 0), ("out", "x", 0)),
    "r0k1": (("up", "xb", 0),),
    "halo!": (("out", "z", 0), ("down", "zb", 1), ("mix", "x", 0), ("mix", "x", 1)),
    "n1b": (("up", "zb", 1),),
    "drain": (("mix", "x", 2), ("mix", "z", 0), ("down", "xb", 0), ("pk", "chip"), ("mix", "z", 1), ("mix", "x", 3), ("pk", "x"), ("mix", "z", 2), ("out", "zb", 0), ("down", "xb", 1), ("mix", "z", 3), ("pk", "z"), ("up", "xb", 1), ("mix", "zb", 0), ("mix", "zb", 1), ("mix", "zb", 2), ("out", "xb", 0), ("mix", "zb", 3), ("mix", "xb", 0), ("mix", "xb", 1), ("mix", "xb", 2), ("mix", "xb", 3)),
}
GELU_A = 0.7978845608028654
GELU_B = 0.044715


def dot(left, right, dims=(1, 0)):
    return lax.dot_general(left, right, ((dims[:1], dims[1:]), ((), ())), preferred_element_type=F32)


def rows_of(block, width):
    return block.reshape(-1, width)


class Wires:
    def __init__(self, send, recv):
        self.send, self.recv, self.used = send, recv, 0

    def copy(self, src, dst, device):
        k = self.used
        self.used += 1
        return pltpu.make_async_remote_copy(
            src_ref=src, dst_ref=dst, send_sem=self.send.at[k], recv_sem=self.recv.at[k],
            device_id=device, device_id_type=MESH,
        )


def block_kernel(
    sizes, long_ref, short_ref, x_hbm, cot_hbm, prev_ref, bias_ref, gain1_ref, taps_ref, gain2_ref, mix_hbm, outw_hbm, up_hbm,
    down_hbm,
    output_hbm, igrad_hbm, finals_ref, small_ref, fin_up, fin_down, fin_out, fin_mix,
    xb, cb, n1h, res, gn2, fo, conv, n2, gm, act, gup, sig, st, ab, sp, sl,
    mix, outw, up, down,
    p_up, p_down, p_out,
    rc_up, ry_up, kx_up, rx_up, rz_up,
    rc_down, ry_down, kx_down, rx_down, rz_down,
    rc_out, ry_out, kx_out, rx_out, rz_out,
    ry_mix, kx_mix, rx_mix, rz_mix,
    prev, biases, halo1, halo2, endrow, endin, brow, bin_, fsend, frecv,
    acc_n1, acc_n2, acc_t, acc_b, pk, pk_core, pk_chip, pk_x, pk_z,
    send_sem, recv_sem, local_sem,
):
    n, z_count, tokens, width, hs, fs, slots, rim = sizes
    chips = n // 2
    steps = tokens // LANES
    tile = 256
    tiles = tokens // tile
    me = lax.axis_index("tensor")
    q, c = me // 2, me % 2
    dp = lax.axis_index("dp")
    z, x = dp // 2, dp % 2
    wires = Wires(send_sem, recv_sem)
    started = []

    def tensor(j):
        return (dp, j)

    sibling = tensor(me + 1 - 2 * c)
    partner = (dp + 1 - 2 * x, me)

    def z_peer(d):
        return ((((z + d) % z_count) * 2) + x, me)

    def shard_of(d, core):
        return ((q + d) % chips) * 2 + core

    def go(copy):
        copy.start()
        started.append(copy)
        return copy

    locals_ = [
        (mix_hbm.at[0], ab.at[0, pl.ds(0, width)]), (mix_hbm.at[1], ab.at[0, pl.ds(width, width)]),
        (outw_hbm, gn2.at[pl.ds(0, hs)]), (up_hbm, fo.at[pl.ds(0, width)]), (down_hbm, fo.at[pl.ds(width, fs)]),
    ]
    loads = [pltpu.make_async_copy(s, d, local_sem.at[i]) for i, (s, d) in enumerate(locals_)]

    def run(ref, g):
        return ref.at[pl.ds(g * steps, steps)]

    x_loads = [pltpu.make_async_copy(run(x_hbm, g), xb.at[:, g, :], local_sem.at[5 + g]) for g in range(LANES)]
    cot_loads = [pltpu.make_async_copy(run(cot_hbm, g), cb.at[:, g, :], local_sem.at[5 + LANES + g]) for g in range(LANES)]
    for copy in loads[:2] + x_loads + loads[2:] + cot_loads:
        copy.start()

    barrier = pltpu.get_barrier_semaphore()
    peers = [tensor((me + d) % n) for d in range(1, n)] + [partner] + [z_peer(d) for d in range(1, z_count)]
    for peer in peers:
        pl.semaphore_signal(barrier, inc=1, device_id=peer, device_id_type=MESH)

    long_count, short_count = long_ref[0], short_ref[0]
    is_long = jnp.where(me < 2 * long_count, 1.0, 0.0)
    in_row = jnp.where(me < 2 * long_count + short_count, 1.0, 0.0)
    odd = (me % 2).astype(F32)
    joined = is_long * odd
    joins_next = is_long * (1.0 - odd)
    starts = in_row * (1.0 - joined)
    ends = in_row * (1.0 - joins_next)
    slot = jnp.where(me < 2 * long_count, me // 2, me - long_count)
    slot_mask = [jnp.where(slot == s, 1.0, 0.0) for s in range(slots)]

    gathers = {}

    def gather(name, ref):
        size = ref.shape[1] // 2
        far, across, passed = [], [], []
        for k in range(size):
            mine, r = ref.at[me, x * size + k], shard_of(1, c)
            ours, theirs = ref.at[r, x * size + k], ref.at[r, (1 - x) * size + k]
            far.append(go(wires.copy(mine, mine, tensor(r))))
            across.append(wires.copy(ours, ours, partner))
            passed.append((wires.copy(ours, ours, sibling), wires.copy(theirs, theirs, sibling)))
        sib = go(wires.copy(ref.at[me], ref.at[me], sibling))
        gathers[name] = (sib, far, across, passed)

    def gather_far(name, k):
        _, far, across, passed = gathers[name]
        far[k].wait_recv()
        go(across[k])
        go(passed[k][0])

    def gather_across(name, k):
        _, far, across, passed = gathers[name]
        across[k].wait_recv()
        go(passed[k][1])

    def gather_passed(name):
        for one, two in gathers[name][3]:
            one.wait_recv()
            two.wait_recv()

    stages = {("g", "far"): gather_far, ("g", "across"): gather_across}

    def run_stages(hook):
        for step in SCHEDULE.get(hook, ()):
            if step[0] == "g":
                stages["g", step[2]](step[1], *step[3:])
            else:
                stages[step[:2]](*step[2:])

    prev[me] = prev_ref[...]
    biases[me] = bias_ref[...]
    loads[0].wait()
    loads[1].wait()
    half = width // 2
    for h in range(2):
        mix[me, pl.ds(2 * h, 2)] = (
            jnp.concatenate([ab[0, pl.ds(h * half, half), :], ab[0, pl.ds(width + h * half, half), :]], axis=1)
            .astype(BF16)
            .reshape((2,) + mix.shape[2:])
        )
    pl.semaphore_wait(barrier, len(peers))
    gather("mix", mix)
    lead_copies = []
    for ref in (prev, biases):
        lead_copies += [go(wires.copy(ref.at[me], ref.at[me], tensor((me + d) % n))) for d in range(1, n)]
    loads[2].wait()
    outw[me] = gn2[pl.ds(0, hs), :].astype(BF16).reshape(2, hs // 2, width)
    gather("out", outw)
    loads[3].wait()
    up[me] = fo[pl.ds(0, width), :].astype(BF16).reshape(up.shape[1:])
    gather("up", up)
    loads[4].wait()
    down[me] = fo[pl.ds(width, fs), :].astype(BF16).reshape(down.shape[1:])
    gather("down", down)

    span = 64
    spans = tokens // span

    def at(i, shift=0, size=span):
        return pl.ds(pl.multiple_of(i * size + shift, LANES), size)

    def take(ref, i, size=span):
        return ref[pl.ds(i * (size // LANES), size // LANES)].reshape(size, width)

    def put(ref, i, value):
        ref[pl.ds(i * (span // LANES), span // LANES)] = value.reshape(span // LANES, LANES, width)

    def eights(value):
        return jnp.sum(value.reshape(-1, LANES, value.shape[-1]), axis=0)

    hook = run_stages
    for copy in x_loads:
        copy.wait()
    gain1 = gain1_ref[...]
    gain2 = gain2_ref[...]

    @pl.loop(0, spans, unroll=4)
    def _(i):
        v = take(xb, i)
        scale = lax.rsqrt(jnp.mean(v * v, axis=-1, keepdims=True) + epsilon)
        n1h[at(i, rim * LANES), :] = v * scale * gain1

    hook("norm1")
    edge = rim * LANES
    halo_copy = go(wires.copy(n1h.at[pl.ds(tokens, edge)], halo1, sibling))
    halo_copy.wait_recv()
    sub = lax.broadcasted_iota(jnp.int32, (LANES, width), 0)
    for k in range(rim):
        own = pltpu.roll(n1h[pl.ds(tokens + k * LANES, LANES), :], 1, 0)
        other = pltpu.roll(halo1[pl.ds(k * LANES, LANES), :], 1, 0)
        n1h[pl.ds(k * LANES, LANES), :] = jnp.where(sub == 0, joined * other, own)
    tap = [taps_ref[pl.ds(k, 1), :] * (1.0 if k == 0 else in_row) for k in range(rim + 1)]

    @pl.loop(0, spans, unroll=4)
    def _(i):
        total = tap[0] * n1h[at(i, edge), :]
        for k in range(1, rim + 1):
            total = total + tap[k] * n1h[at(i, edge - k * LANES), :]
        conv[at(i), :] = total.astype(BF16)

    def project(j):
        weight = rows_of(mix[j], 2 * hs)
        bias = biases[j]

        @pl.loop(0, tiles, unroll=tiles)
        def _(t):
            rows = at(t, 0, tile)
            pre = dot(conv[rows, :], weight)
            logit = pre[:, :hs] + bias
            cand = pre[:, hs:]
            e = jnp.exp(-jnp.abs(logit))
            r = 1.0 / (1.0 + e)
            opened = jnp.where(logit >= 0, r, e * r)
            keep = jnp.where(logit >= 0, e * r, r)
            soft = jnp.maximum(cand, 0.0) + jnp.log1p(jnp.exp(-jnp.abs(cand)))
            sig[j, rows, :] = opened
            sp[j, rows, :] = soft
            ab[j, rows, :] = keep * in_row
            st[j, at(t, LANES, tile), :] = opened * soft

    hook("conv")
    for copy in lead_copies:
        copy.wait_recv()
    project(me)
    hook("own")
    gathers["mix"][0].wait_recv()
    project(me + 1 - 2 * c)
    hook("sib")

    def unrolled(count, step, carry, by=4):
        def some(i, carry):
            for k in range(by):
                carry = step(i * by + k, carry)
            return carry

        return lax.fori_loop(0, count // by, some, carry)

    one = jnp.ones((LANES, hs), F32)
    zero = jnp.zeros((LANES, hs), F32)

    def scan(js):
        def step(s, carry):
            rows = at(s, 0, LANES)
            later = at(s, LANES, LANES)
            out = []
            for j, (fac, val) in zip(js, carry):
                a = ab[j, rows, :]
                fac = a * fac
                val = a * val + st[j, later, :]
                ab[j, rows, :] = fac
                st[j, later, :] = val
                out.append((fac, val))
            return tuple(out)

        unrolled(steps, step, tuple((one, zero) for _ in js))

    scan([me, me + 1 - 2 * c])
    hook("scan1")
    for copy in cot_loads:
        copy.wait()

    @pl.loop(0, spans, unroll=4)
    def _(i):
        gm[at(i), :] = (in_row * take(cb, i)).astype(BF16)

    hook("gm")
    hook("mixfar!")
    project(shard_of(1, c))
    hook("rown")
    hook("mixpass!")
    gather_passed("mix")
    project(shard_of(1, 1 - c))
    hook("rsib")
    scan([shard_of(1, c), shard_of(1, 1 - c)])
    hook("scan2")
    last = pl.ds(tokens - LANES, LANES)

    def chain(j, carry, keep_rows):
        fac = ab[j, last, :]
        val = st[j, pl.ds(tokens, LANES), :]
        rows = []
        for g in range(LANES):
            rows.append(carry)
            carry = fac[g : g + 1] * carry + val[g : g + 1]
        if keep_rows:
            st[j, pl.ds(0, LANES), :] = jnp.concatenate(rows, axis=0)
        return carry

    first = []
    for j in range(n):
        begin = jnp.zeros((1, hs), F32)
        for s in range(slots):
            begin = begin + (starts * slot_mask[s]) * prev[j, pl.ds(s, 1), :]
        first.append(begin)
        endrow[j] = chain(j, begin, False)
    end_copy = go(wires.copy(endrow, endin, sibling))
    hook("chain")
    hook("end!")
    end_copy.wait_recv()
    for j in range(n):
        ending = chain(j, first[j] + joined * endin[j], True)
        for s in range(slots):
            fsend[j, pl.ds(s, 1), :] = (ends * slot_mask[s]) * ending
    final_copies = [
        go(wires.copy(fsend.at[(me + d) % n], frecv.at[d - 1], tensor((me + d) % n))) for d in range(1, n)
    ]

    hook("chain2")
    hook("out!")
    gathers["out"][0].wait_recv()
    gather_passed("out")
    @pl.loop(0, tiles, unroll=tiles)
    def _(t):
        rows = at(t, 0, tile)
        mixed = jnp.zeros((tile, width), F32)
        for j in range(n):
            into = st[j, pl.ds(0, LANES), :]
            value = st[j, at(t, LANES, tile), :] + (
                ab[j, rows, :].reshape(-1, LANES, hs) * into[None]
            ).reshape(tile, hs)
            st[j, at(t, LANES, tile), :] = value
            low = value.astype(BF16)
            sl[j, rows, :] = low
            mixed = mixed + dot(low, rows_of(outw[j], width))
        resid = take(xb, t, tile) + in_row * mixed
        res[rows, :] = resid
        scale = lax.rsqrt(jnp.mean(resid * resid, axis=-1, keepdims=True) + epsilon)
        n2[rows, :] = (resid * scale * gain2).astype(BF16)

    hook("states")
    hook("updown!")
    gather_passed("up")
    gather_passed("down")
    gathers["up"][0].wait_recv()
    gathers["down"][0].wait_recv()
    sent_weights = list(started)

    class Sum:
        def __init__(self, part, rc, ry, kx, rx, rz, fin):
            self.part, self.rc, self.ry, self.kx, self.rx, self.rz, self.fin = part, rc, ry, kx, rx, rz, fin
            self.chunks = fin.shape[0]
            self.c1 = [None] * chips
            self.c2, self.c3, self.c4, self.c5, self.c6 = {}, {}, {}, {}, {}
            self.first = wires.used
            wires.used += chips

        def one(self, d):
            copy = pltpu.make_async_remote_copy(
                src_ref=self.part.at[shard_of(d, 1 - c)], dst_ref=self.rc.at[d], send_sem=send_sem.at[self.first + d],
                recv_sem=recv_sem.at[self.first + d], device_id=sibling, device_id_type=MESH,
            )
            self.c1[d] = go(copy)

        def both(self, j, d, k, h):
            return self.part[j, k, h].astype(F32) + self.rc[d, k, h].astype(F32)

        def y(self, k=0):
            self.c2[k] = []
            for d in range(1, chips):
                if k == 0:
                    self.c1[d].wait_recv()
                j = shard_of(d, c)
                for h in range(2):
                    self.part[j, k, h] = self.both(j, d, k, h).astype(BF16)
                self.c2[k].append(go(wires.copy(self.part.at[j, k], self.ry.at[d - 1, k], tensor(j))))

        def total(self, k, h):
            v = self.both(me, 0, k, h)
            for d in range(chips - 1):
                v = v + self.ry[d, k, h].astype(F32)
            return v

        def x(self, k=0):
            if k == 0:
                self.c1[0].wait_recv()
            for copy in self.c2[k]:
                copy.wait_recv()
            self.part[me, k, 1 - x] = self.total(k, 1 - x).astype(BF16)
            self.c3[k] = go(wires.copy(self.part.at[me, k, 1 - x], self.rx.at[k], partner))
            self.kx[k] = self.total(k, x)

        def z(self, k=0):
            self.c3[k].wait_recv()
            self.spread(k, self.kx[k] + self.rx[k].astype(F32))

        def spread(self, k, v):
            self.kx[k] = v
            self.part[me, k, x] = v.astype(BF16)
            self.c4[k] = [
                go(wires.copy(self.part.at[me, k, x, (z + d) % z_count], self.rz.at[d - 1, k], z_peer(d)))
                for d in range(1, z_count)
            ]

        def zb(self, k=0):
            for copy in self.c4[k]:
                copy.wait_recv()
            v = self.kx[k, z]
            for d in range(z_count - 1):
                v = v + self.rz[d, k].astype(F32)
            self.fin[k, x, z] = v.astype(BF16)
            mine = self.fin.at[k, x, z]
            self.c5[k] = [go(wires.copy(mine, mine, z_peer(d))) for d in range(1, z_count)]
            self.c6[k] = [go(wires.copy(mine, mine, partner))]

        def xb(self, k=0):
            for d in range(1, z_count):
                self.c5[k][d - 1].wait_recv()
                theirs = self.fin.at[k, x, (z + z_count - d) % z_count]
                self.c6[k].append(go(wires.copy(theirs, theirs, partner)))

        def end(self):
            for k in range(self.chunks):
                for copy in self.c6[k]:
                    copy.wait_recv()

    class SumAcross(Sum):
        def xa(self, d, k=0):
            if k == 0:
                self.c1[d].wait_recv()
            j = shard_of(d, c)
            self.part[j, k, 1 - x] = self.both(j, d, k, 1 - x).astype(BF16)
            self.c3[d, k] = go(wires.copy(self.part.at[j, k, 1 - x], self.rx.at[d, k], partner))

        def ya(self, k=0):
            self.c3[1, k].wait_recv()
            j = shard_of(1, c)
            self.part[j, k, x] = (self.both(j, 1, k, x) + self.rx[1, k].astype(F32)).astype(BF16)
            self.c2[k] = go(wires.copy(self.part.at[j, k, x], self.ry.at[k], tensor(j)))

        def z(self, k=0):
            self.c3[0, k].wait_recv()
            self.c2[k].wait_recv()
            self.spread(k, self.both(me, 0, k, x) + self.rx[0, k].astype(F32) + self.ry[k].astype(F32))

    s_up = Sum(p_up, rc_up, ry_up, kx_up, rx_up, rz_up, fin_up)
    s_down = SumAcross(p_down, rc_down, ry_down, kx_down, rx_down, rz_down, fin_down)
    s_out = Sum(p_out, rc_out, ry_out, kx_out, rx_out, rz_out, fin_out)
    s_mix = Sum(up, down, ry_mix, kx_mix, rx_mix, rz_mix, fin_mix)

    for name, unit in (("up", s_up), ("down", s_down), ("out", s_out), ("mix", s_mix)):
        for stage in ("y", "x", "xa", "ya", "z", "zb", "xb"):
            stages[name, stage] = getattr(unit, stage, None)

    def weight_grad(unit, j, left, right):
        unit.part[j] = dot(left, right, (0, 0)).astype(BF16).reshape(unit.part.shape[1:])

    def feed(j, begin, name):
        def some(t):
            rows = at(t, 0, tile)
            upw = rows_of(up[j], fs)
            downw = rows_of(down[j], width)
            u = dot(n2[rows, :], upw)
            ga = dot(gm[rows, :], downw, (1, 1))
            u2 = u * u
            th = jnp.tanh(GELU_A * u * (1.0 + GELU_B * u2))
            hp = 0.5 + 0.5 * th
            a = (u * hp).astype(BF16)
            slope = hp + (0.5 * GELU_A) * u * (1.0 - th * th) * (1.0 + 3.0 * GELU_B * u2)
            gu = (ga * slope).astype(BF16)
            act[rows, :] = a
            gup[rows, :] = gu
            o = dot(a, downw)
            g = dot(gu, upw, (1, 1))
            if begin:
                fo[rows, :] = o
                gn2[rows, :] = g
            else:
                fo[rows, :] = fo[rows, :] + o
                gn2[rows, :] = gn2[rows, :] + g

        half_tiles = tiles // 2
        pl.loop(0, half_tiles, unroll=half_tiles)(some)
        hook(name + "a")
        pl.loop(half_tiles, tiles, unroll=half_tiles)(some)
        hook(name + "b")
        weight_grad(s_up, j, n2[...], gup[...])
        hook(name + "u")
        weight_grad(s_down, j, gm[...], act[...])
        hook(name + "d")

    feed(shard_of(1, 1 - c), True, "f0")
    s_up.one(1)
    s_down.one(1)
    hook("f0e")
    feed(shard_of(1, c), False, "f1")
    hook("f1e")
    feed(me + 1 - 2 * c, False, "f2")
    s_up.one(0)
    s_down.one(0)
    hook("f2e")
    feed(me, False, "f3")
    hook("f3e")

    acc_n2[...] = jnp.zeros_like(acc_n2)

    def norm2_back(i):
        r = res[at(i), :]
        g = gn2[at(i), :]
        scale = lax.rsqrt(jnp.mean(r * r, axis=-1, keepdims=True) + epsilon)
        gg = g * gain2
        m = jnp.mean(gg * r, axis=-1, keepdims=True)
        gr = take(cb, i) + scale * gg - r * (scale * scale * scale * m)
        acc_n2[...] += eights(g * r * scale)
        gn2[at(i), :] = gr
        gm[at(i), :] = (in_row * gr).astype(BF16)
        put(cb, i, r + in_row * fo[at(i), :])

    pl.loop(0, spans // 2, unroll=2)(norm2_back)
    hook("B1a")
    pl.loop(spans // 2, spans, unroll=2)(norm2_back)
    hook("B1b")

    def store(ref, hbm, first):
        copies = [pltpu.make_async_copy(ref.at[:, g, :], run(hbm, g), local_sem.at[first + g]) for g in range(LANES)]
        for copy in copies:
            copy.start()
        return copies

    stores = store(cb, output_hbm, 5 + 2 * LANES)
    for copy in sent_weights:
        copy.wait_send()
        started.remove(copy)

    for d in (1, 0):
        for core in (1 - c, c):
            j = shard_of(d, core)
            weight_grad(s_out, j, gm[...], sl[j])
        s_out.one(d)
        hook(f"og{d}")
    hook("oge")

    for j in range(n):
        acc_b[j] = jnp.zeros((LANES, hs), F32)

    def recur_back(d, begin, name):
        js = [shard_of(d, core) for core in range(2)]
        for k in range(2):
            ab[k] = dot(gm[...], rows_of(outw[js[k]], width), (1, 1))
        hook(name + "g")

        def back_step(i, carry):
            s = steps - 1 - i
            rows = at(s, 0, LANES)
            out = []
            for k in range(2):
                fac, val, keep = carry[k]
                fac = keep * fac
                val = ab[k, rows, :] + keep * val
                ab[2 + k, rows, :] = fac
                ab[k, rows, :] = val
                out.append((fac, val, 1.0 - sig[js[k], rows, :]))
            return tuple(out)

        unrolled(steps, back_step, ((one, zero, one), (one, zero, one)))
        hook(name + "s")

        def chain_back(k, carry):
            fac = ab[2 + k, pl.ds(0, LANES), :]
            val = ab[k, pl.ds(0, LANES), :]
            keep = 1.0 - sig[js[k], pl.ds(0, LANES), :]
            rows = []
            for g in reversed(range(LANES)):
                rows.append(carry)
                carry = keep[g : g + 1] * (val[g : g + 1] + fac[g : g + 1] * carry)
            return carry, jnp.concatenate(rows[::-1], axis=0)

        slot_ = 2 * d
        for k in range(2):
            brow[slot_ + k] = chain_back(k, jnp.zeros((1, hs), F32))[0]
        copy = go(wires.copy(brow.at[pl.ds(slot_, 2)], bin_.at[pl.ds(slot_, 2)], sibling))
        hook(name + "c")
        hook(name + "w!")
        copy.wait_recv()
        for k in (0, 1):
            j = js[k]
            into = chain_back(k, joins_next * bin_[slot_ + k])[1]
            weight = rows_of(mix[j], 2 * hs)

            @pl.loop(0, tiles, unroll=tiles)
            def _(t, j=j, k=k, into=into, weight=weight):
                rows = at(t, 0, tile)
                carried = ab[k, rows, :] + (ab[2 + k, rows, :].reshape(-1, LANES, hs) * into[None]).reshape(tile, hs)
                opened = sig[j, rows, :]
                soft = sp[j, rows, :]
                weighted = carried * opened
                gl = weighted * (soft - st[j, rows, :]) * (1.0 - opened)
                close = jnp.where(soft < 0.01, soft * (1.0 - soft * (0.5 - soft * (1.0 / 6.0))), 1.0 - jnp.exp(-soft))
                gc = weighted * close
                acc_b[j] += eights(gl)
                gp = jnp.concatenate([gl.astype(BF16), gc.astype(BF16)], axis=1)
                act[rows, :] = gp
                back = dot(gp, weight, (1, 1))
                if begin and k == 0:
                    res[rows, :] = back
                else:
                    res[rows, :] = res[rows, :] + back

            hook(f"{name}k{k}")
            weight_grad(s_mix, j, conv[...], act[...])
            hook(f"{name}w{k}")

    recur_back(1, True, "r1")
    s_mix.one(1)
    hook("r1e")
    recur_back(0, False, "r0")
    s_mix.one(0)
    hook("r0e")
    halo_back = go(wires.copy(res.at[pl.ds(0, edge)], halo2, sibling))
    hook("h0")
    hook("halo!")
    halo_back.wait_recv()

    for k in range(rim):
        own = pltpu.roll(res[pl.ds(k * LANES, LANES), :], LANES - 1, 0)
        other = pltpu.roll(halo2[pl.ds(k * LANES, LANES), :], LANES - 1, 0)
        res[pl.ds(tokens + k * LANES, LANES), :] = jnp.where(sub == LANES - 1, joins_next * other, own)
    acc_n1[...] = jnp.zeros_like(acc_n1)
    acc_t[...] = jnp.zeros_like(acc_t)

    def norm1_back(i):
        g0 = res[at(i), :]
        total = tap[0] * g0
        acc_t[0] += eights(g0 * n1h[at(i, edge), :])
        for k in range(1, rim + 1):
            total = total + tap[k] * res[at(i, k * LANES), :]
            acc_t[k] += eights(g0 * n1h[at(i, edge - k * LANES), :])
        v = take(xb, i)
        scale = lax.rsqrt(jnp.mean(v * v, axis=-1, keepdims=True) + epsilon)
        gg = total * gain1
        m = jnp.mean(gg * v, axis=-1, keepdims=True)
        acc_n1[...] += eights(total * v * scale)
        put(xb, i, gn2[at(i), :] + scale * gg - v * (scale * scale * scale * m))

    pl.loop(0, spans // 2, unroll=2)(norm1_back)
    hook("n1a")
    pl.loop(spans // 2, spans, unroll=2)(norm1_back)
    stores += store(xb, igrad_hbm, 5 + 3 * LANES)
    hook("n1b")

    pk[...] = jnp.zeros_like(pk)
    pk[pl.ds(0, 1), :] = jnp.sum(acc_n1[...], axis=0, keepdims=True)
    for k in range(rim + 1):
        pk[pl.ds(1 + k, 1), :] = jnp.sum(acc_t[k], axis=0, keepdims=True)
    pk[pl.ds(6, 1), :] = jnp.sum(acc_n2[...], axis=0, keepdims=True)
    for j in range(n):
        pk[pl.ds(8 + j, 1), pl.ds(0, hs)] = jnp.sum(acc_b[j], axis=0, keepdims=True)
    k1 = go(wires.copy(pk, pk_core, sibling))
    small_copies = {}

    def small_chip():
        k1.wait_recv()
        pk_chip[q] = pk[...] + pk_core[...]
        small_copies[2] = go(wires.copy(pk_chip.at[q], pk_chip.at[q], tensor(shard_of(1, c))))

    def small_x():
        small_copies[2].wait_recv()
        pk_x[0] = pk_chip[0] + pk_chip[1]
        small_copies[3] = go(wires.copy(pk_x.at[0], pk_x.at[1], partner))

    def small_z():
        small_copies[3].wait_recv()
        pk_z[z] = pk_x[0] + pk_x[1]
        small_copies[4] = [go(wires.copy(pk_z.at[z], pk_z.at[z], z_peer(d))) for d in range(1, z_count)]

    stages["pk", "chip"], stages["pk", "x"], stages["pk", "z"] = small_chip, small_x, small_z
    hook("pk")
    hook("drain")
    for copy in final_copies:
        copy.wait_recv()
    total = fsend[me]
    for d in range(n - 1):
        total = total + frecv[d]
    finals_ref[...] = total
    for copy in small_copies[4]:
        copy.wait_recv()
    value = pk_z[0]
    for k in range(1, z_count):
        value = value + pk_z[k]
    small_ref[...] = value
    for unit in (s_up, s_down, s_out, s_mix):
        unit.end()
    for copy in started:
        copy.wait_send()
    for copy in stores:
        copy.wait()


def last_kernel(
    hs, output_in, igrad_in, finals_in, small, g_up, g_down, g_out, g_mix,
    output, finals, igrad, gain1, taps, mixer, bias, outw, gain2, up, down, big_a, big_b, mixer_v, outw_v, up_v, down_v, sem,
):
    width = up_v.shape[0]
    first = [pltpu.make_async_copy(output_in, big_a, sem.at[0]), pltpu.make_async_copy(igrad_in, big_b, sem.at[1])]
    for copy in first:
        copy.start()
    me = lax.axis_index("tensor")
    up_v[...] = rows_of(g_up[...], up_v.shape[1]).astype(F32)
    later = [pltpu.make_async_copy(up_v, up, sem.at[2])]
    later[-1].start()
    for copy, src, dst, k in zip(first, (big_a, big_b), (output, igrad), (3, 4)):
        copy.wait()
        later.append(pltpu.make_async_copy(src, dst, sem.at[k]))
        later[-1].start()
    both = rows_of(g_mix[...], 2 * hs).astype(F32)
    mixer_v[0] = both[:, :hs]
    mixer_v[1] = both[:, hs:]
    later.append(pltpu.make_async_copy(mixer_v, mixer, sem.at[5]))
    later[-1].start()
    down_v[...] = rows_of(g_down[...], width).astype(F32).T
    later.append(pltpu.make_async_copy(down_v, down, sem.at[6]))
    later[-1].start()
    outw_v[...] = rows_of(g_out[...], hs).astype(F32).T
    later.append(pltpu.make_async_copy(outw_v, outw, sem.at[7]))
    later[-1].start()
    finals[...] = finals_in[...]
    gain1[...] = small[pl.ds(0, 1), :]
    taps[...] = small[pl.ds(1, taps.shape[0]), :]
    gain2[...] = small[pl.ds(6, 1), :]
    bias[...] = small[pl.ds(8 + me, 1), pl.ds(0, hs)]
    for copy in later:
        copy.wait()


def fused(
    block_input, long_rows, short_rows, prev_states, norm1_gain, conv_weight, mixer_weight, gate_bias,
    out_weight, norm2_gain, up_weight, down_weight, cotangent,
):
    tokens, width = block_input.shape
    n = lax.axis_size("tensor")
    z_count = lax.axis_size("dp") // 2
    chips = n // 2
    slots, hs = prev_states.shape
    fs = up_weight.shape[1]
    rim = conv_weight.shape[0] - 1
    steps = tokens // LANES
    pk_rows = 8 + -(-n // 8) * 8
    units = [(CHUNKS[0], fs), (CHUNKS[1], fs), (CHUNKS[2], hs), (CHUNKS[3], 2 * hs)]

    def block(chunks, cols):
        return (chunks, 2, z_count, width // (2 * z_count * chunks), cols)

    def full(chunks, cols):
        return pltpu.VMEM((n,) + block(chunks, cols), BF16)

    def sums(chunks, cols, across=False):
        dims = block(chunks, cols)
        part = dims[2:]
        return [
            pltpu.VMEM((chips,) + dims, BF16),
            pltpu.VMEM((chunks,) + part if across else (chips - 1,) + dims, BF16),
            pltpu.VMEM((chunks,) + part, F32),
            pltpu.VMEM(((chips, chunks) if across else (chunks,)) + part, BF16),
            pltpu.VMEM((z_count - 1, chunks) + part[1:], BF16),
        ]

    def wide(rows, kind=F32):
        return pltpu.VMEM((rows, width), kind)

    permuted = pltpu.VMEM((steps, LANES, width), F32)
    per_block = pltpu.VMEM((n, tokens, hs), F32)
    scratch = [
        permuted, permuted, wide(tokens + rim * LANES), wide(tokens + rim * LANES), wide(tokens), wide(tokens),
        wide(tokens, BF16), wide(tokens, BF16), wide(tokens, BF16), pltpu.VMEM((tokens, fs), BF16), pltpu.VMEM((tokens, fs), BF16),
        per_block, pltpu.VMEM((n, tokens + LANES, hs), F32), per_block, per_block, pltpu.VMEM((n, tokens, hs), BF16),
        pltpu.VMEM((n, 4, width // 4, 2 * hs), BF16), pltpu.VMEM((n, 2, hs // 2, width), BF16), full(*units[3]), full(*units[3]),
        *[full(*unit) for unit in units[:3]],
        *sums(*units[0]), *sums(*units[1], True), *sums(*units[2]), *sums(*units[3])[1:],
        pltpu.VMEM((n, slots, hs), F32), pltpu.VMEM((n, 1, hs), F32), wide(rim * LANES), wide(rim * LANES),
        pltpu.VMEM((n, 1, hs), F32), pltpu.VMEM((n, 1, hs), F32), pltpu.VMEM((n, 1, hs), F32), pltpu.VMEM((n, 1, hs), F32),
        pltpu.VMEM((n, slots, hs), F32), pltpu.VMEM((n - 1, slots, hs), F32),
        wide(LANES), wide(LANES), pltpu.VMEM((rim + 1, LANES, width), F32), pltpu.VMEM((n, LANES, hs), F32),
        wide(pk_rows), wide(pk_rows), pltpu.VMEM((chips, pk_rows, width), F32), pltpu.VMEM((2, pk_rows, width), F32),
        pltpu.VMEM((z_count, pk_rows, width), F32),
        pltpu.SemaphoreType.DMA((WIRES,)), pltpu.SemaphoreType.DMA((WIRES,)), pltpu.SemaphoreType.DMA((5 + 4 * LANES,)),
    ]
    vmem = pl.BlockSpec(memory_space=pltpu.VMEM)
    smem = pl.BlockSpec(memory_space=pltpu.SMEM)
    hbm = pl.BlockSpec(memory_space=pl.ANY)

    def shape(dims, kind=F32):
        return jax.ShapeDtypeStruct(dims, kind)

    big = shape((tokens, width))
    outs = pl.pallas_call(
        functools.partial(block_kernel, (n, z_count, tokens, width, hs, fs, slots, rim)),
        out_shape=[big, big, shape((slots, hs)), shape((pk_rows, width)), *[shape(block(*unit), BF16) for unit in units]],
        in_specs=[smem, smem, hbm, hbm, vmem, vmem, vmem, vmem, vmem, hbm, hbm, hbm, hbm],
        out_specs=[hbm, hbm] + [vmem] * 6,
        scratch_shapes=scratch,
        compiler_params=pltpu.CompilerParams(collective_id=0, has_side_effects=True, vmem_limit_bytes=VMEM_LIMIT),
    )(
        long_rows, short_rows, block_input, cotangent, prev_states, gate_bias[None], norm1_gain[None], conv_weight,
        norm2_gain[None], mixer_weight, out_weight, up_weight, down_weight,
    )
    outs = pl.pallas_call(
        functools.partial(last_kernel, hs),
        out_shape=[
            big, shape((slots, hs)), big, shape((1, width)), shape((rim + 1, width)), shape((2, width, hs)), shape((1, hs)),
            shape((hs, width)), shape((1, width)), shape((width, fs)), shape((fs, width)),
        ],
        in_specs=[hbm, hbm] + [vmem] * 6,
        out_specs=[hbm, vmem, hbm, vmem, vmem, hbm, vmem, hbm, vmem, hbm, hbm],
        scratch_shapes=[
            wide(tokens), wide(tokens), pltpu.VMEM((2, width, hs), F32), wide(hs), pltpu.VMEM((width, fs), F32), wide(fs),
            pltpu.SemaphoreType.DMA((8,)),
        ],
        compiler_params=pltpu.CompilerParams(vmem_limit_bytes=VMEM_LIMIT),
    )(*outs)
    output, finals, input_grad, gain1, taps, mixer, bias, outw, gain2, up, down = outs
    return (output, finals, input_grad, gain1[0], taps, mixer, bias[0], outw, gain2[0], up, down)


def solution(mesh):
    takes_kernel = mesh.shape["tensor"] == 4 and mesh.shape["dp"] == 8
    rows = P(("dp", "tensor"), None)
    placed = (
        rows, P("dp"), P("dp"), P("dp", "tensor"), P(), P(), P(None, None, "tensor"), P("tensor"),
        P("tensor", None), P(), P(None, "tensor"), P("tensor", None), rows,
    )
    return jax.shard_map(
        fused if takes_kernel else plain,
        mesh=mesh,
        in_specs=placed,
        out_specs=(
            rows, P("dp", "tensor"), rows, P(), P(), P(None, None, "tensor"), P("tensor"), P("tensor", None),
            P(), P(None, "tensor"), P("tensor", None),
        ),
        check_vma=False,
    )
```

time: 157 us -> 126 us (0.80)
  Pallas kernels: 139 us -> 124 us
  local copies, waits for them, and re-layouts: 10.5 us -> 0 us
  other arithmetic: 4.82 us -> 0 us
    pallas_call x1, Pallas kernels: 139 us -> 117 us  [fused(): pl.pallas_call(functools.partial(block_kernel, (n, z_count, tokens, width...]
    pallas_call x0 -> x1, Pallas kernels: none -> 6.93 us  [fused(): pl.pallas_call(functools.partial(last_kernel, hs), out_shape=[big, shape(...]
    unnamed x15 -> x0, local copies, waits for them, and re-layouts: 4.08 us -> none
    slice x2 -> x0, local copies, waits for them, and re-layouts: 2.7 us -> none  [the longest x1 1.38 us: fused(): small[6]]
    transpose x2 -> x0, other arithmetic: 2.32 us -> none  [fused(): return (output, finals, input_grad, small[0], small[1:2 + rim], mixer_gra...]
    transpose x2 -> x0, local copies, waits for them, and re-layouts: 2.3 us -> none  [fused(): return (output, finals, input_grad, small[0], small[1:2 + rim], mixer_gra...]
where the time goes in v2:
time: 126 us
  Pallas kernels  124 us (98%)
  between operations  2.15 us (2%)
    pallas_call x1, Pallas kernels, fused(): pl.pallas_call(functools.partial(block_kernel, (n, z_count, tokens, width...  117 us
    pallas_call x1, Pallas kernels, fused(): pl.pallas_call(functools.partial(last_kernel, hs), out_shape=[big, shape(...  6.93 us

profile of v2, /device:TPU:0, one launch (start us, length us, event | category | flops | bytes accessed | tf_op | source)
XLA Modules:
  0.0 126.1 jit_solution(14273609852318460579)
XLA Ops:
  1.9 117.0 %shard_map.212 = (f32[1024,512]{1,0:T(8,128)}, f32[1024,512]{1,0:T(8,128)}, f32[4,256]{1,0:T(4,128)}, f32[16,512]{1,0:T(8,128)}, bf16[2,2,4,32,512]{4,3,2,1,0:T(...) custom-call(s32[1]{0:T(128)S(6)} %copy.24.long_ref, ...), custom_call_target="tpu_custom_call" | custom-call | tf_op jit(solution)/shard_map/pallas_call | solution.py:966
  118.9 6.9 %shard_map.213 = (f32[1024,512]{1,0:T(8,128)}, f32[4,256]{1,0:T(4,128)}, f32[1024,512]{1,0:T(8,128)}, f32[1,512]{1,0:T(1,128)}, f32[4,512]{1,0:T(4,128)}, /*inde...) custom-call(f32[1024,512]{1,0:T(8,128)} %get-tuple-element.30.output, ...), custom_call_target="tpu_custom_call" | custom-call | tf_op jit(solution)/shard_map/pallas_call | solution.py:977
